TPU v7x, 256 devices: a whole 4x4x8 slice. The times are simulated.
256 devices in a mesh: occ: 2 (over z_hi), vir: 32 (over z_lo, x, core), pair: 4 (over y).
Axes of the slice: x: 4, y: 4, z: 8 (z_hi: 2, z_lo: 4; z = z_hi * 4 + z_lo), core: 2. Of those that a mesh axis runs over, the one named last changes fastest.
Arguments:
- amplitudes: bfloat16 [2, 1280, 128, 1280], P(None, 'pair', 'vir', 'occ'), may hold values from -6 to 6
- integrals: bfloat16 [128, 1280, 2, 1280], P('vir', 'occ', None, 'pair'), may hold values from -0.01953125 to 0.01953125
- screen: int32 [2, 20, 128, 20], P(None, 'pair', 'vir', 'occ'), may hold values 0 or 1
- occ_energy: float32 [2], replicated, may hold values from -2 to -0.5
- vir_energy: float32 [1280], replicated, may hold values from 0.5 to 3
- owner: int32 [4], replicated, may hold values from 0 to 3, as said below
Outputs:
- residual: float32 [4, 1280, 1280], P('pair', ('occ', 'vir'))
Inputs may be any that keep to these rules, and one draw needn't show every extreme that they name: owner names every ordered pair i * 2 + j once; for i != j the slot of (j, i) is that of (i, j) plus 4 // 2, counted modulo 4.
All inputs are finite; a program needn't handle non-finite values. No bound on the sum of `screen` on one device may be relied on, other than what follows from the above.
Results may differ from a plain program's by a relative error of at most 0.0003.
Values may be sent and summed in bfloat16 or wider, within the bound.
No kernel may reach another device: no remote copies, remote signals or barrier semaphores. Data moves between devices by JAX's collectives and lax.ppermute only.
A program may use at most 128 MiB of HBM per device.

v0:
```python
import jax
import jax.numpy as jnp
from jax import lax
from jax.sharding import PartitionSpec as P


def partner(value, axis, stride):
    mask = 2**stride
    pairs = [(source, source ^ mask) for source in range(lax.axis_size(axis))]
    return lax.ppermute(value, axis, pairs)


def body(amplitudes, integrals, screen, occ_energy, vir_energy, owner):
    batch_count, quarter_rows, occ_local, vir_local = amplitudes.shape
    vir_width = vir_energy.shape[0]
    tile_width = quarter_rows // screen.shape[1]
    expanded = jnp.broadcast_to(
        screen[:, :, None, :, :, None],
        (batch_count, screen.shape[1], tile_width, occ_local, screen.shape[3], tile_width),
    )
    masked = amplitudes * expanded.reshape(amplitudes.shape).astype(jnp.bfloat16)
    my_slot = lax.axis_index("pair")
    pair_combo = owner[my_slot]
    occ_first = pair_combo // batch_count
    occ_second = pair_combo % batch_count
    inner_size = occ_local * vir_local
    gathered = lax.all_gather(masked, "pair", axis=1, tiled=True)
    left_block = lax.dynamic_index_in_dim(gathered, occ_first, 0, keepdims=False).reshape(
        vir_width, inner_size
    )
    segment = lax.all_gather(integrals, "pair", axis=3, tiled=True)
    picked = lax.dynamic_index_in_dim(segment, occ_second, 2, keepdims=False)
    partial_cycle = jnp.dot(
        left_block, picked.reshape(inner_size, segment.shape[3]), preferred_element_type=jnp.float32
    )
    row_block = lax.psum_scatter(partial_cycle, ("occ", "vir"), scatter_dimension=0, tiled=True)
    columns = lax.all_to_all(row_block, ("occ", "vir"), split_axis=1, concat_axis=0, tiled=True)
    swapped = partner(columns, "pair", lax.axis_size("pair").bit_length() - 2)
    mirrored = jnp.where(occ_first == occ_second, columns, swapped).T
    row_count = row_block.shape[0]
    row_start = lax.axis_index(("occ", "vir")) * row_count
    row_energy = lax.dynamic_slice_in_dim(vir_energy, row_start, row_count)
    energy_gap = (
        occ_energy[occ_first] + occ_energy[occ_second] - row_energy[:, None] - vir_energy[None, :]
    )
    return ((row_block + mirrored) / energy_gap)[None]


def solution(mesh):
    return jax.shard_map(
        body,
        mesh=mesh,
        in_specs=(
            P(None, "pair", "vir", "occ"),
            P("vir", "occ", None, "pair"),
            P(None, "pair", "vir", "occ"),
            P(),
            P(),
            P(),
        ),
        out_specs=P("pair", ("occ", "vir"), None),
        check_vma=False,
    )
```

profile of v0, /device:TPU:1, one launch (start us, length us, event | category | flops | bytes accessed | tf_op | source)
XLA Modules:
  0.0 542.7 jit_solution(8036756237461138254)
XLA Ops:
  6.5 6.2 %copy.23 = bf16[4,640,2,320]{1,0,2,3:T(4,128)(2,1)} copy(bf16[4,640,2,320]{1,3,2,0:T(8,128)(2,1)} %param.7) | data formatting | bytes 6553600 | tf_op args[1]
  12.8 5.4 broadcast_in_dim.4
  18.2 11.7 %convert_element_type.8 = bf16[2,320,4,640]{3,1,2,0:T(8,128)(2,1)S(1)} reshape(bf16[2,5,64,4,10,64]{5,4,2,1,3,0:T(8,128)(2,1)} %broadcast_in_dim.4) | data formatting | bytes 6553600 | tf_op jit(solution)/shard_map/convert_element_type | solution.py:21
  29.9 4.8 copy_multiply_fusion
  34.7 0.2 all-reduce.3.cloned.1.call-start
  35.0 0.6 dynamic_slice.20
  38.2 104.1 %all-gather.5.cloned.1.call-done = bf16[4,640,2,1280]{1,0,2,3:T(4,128)(2,1)} async-done(((bf16[4,640,2,320]{1,0,2,3:T(4,128)(2,1)}), bf16[4,640,2,1280]{1,0,2,3:T(4,128)(2,1)}) %all-gather.5.cloned.1.call-update) | async-done | bytes 13107216 | tf_op jit(solution)/shard_map/all_gather | solution.py:31
  142.3 7.9 %constant_dynamic-slice_fusion.1 = bf16[4,640,1,1280]{1,0,2,3:T(4,128)(2,1)} fusion(bf16[4,640,2,1280]{1,0,2,3:T(4,128)(2,1)} %all-gather.5.cloned.1.call-done, s32[]{:T(128)S(6)} %select_n.39), kind=kLoop, calls=%fused_computation.6 | loop fusion | bytes 13107204 | tf_op jit(solution)/shard_map/jit(dynamic_index_in_dim)/dynamic_slice | solution.py:32
  150.2 12.6 %copy.29 = bf16[4,640,1,1280]{3,1,0,2:T(8,128)(2,1)} copy(bf16[4,640,1,1280]{1,0,2,3:T(4,128)(2,1)} %constant_dynamic-slice_fusion.1) | data formatting | bytes 13107200
  162.8 107.9 %all-gather.3.cloned.1.call-done = bf16[2,1280,4,640]{3,1,2,0:T(8,128)(2,1)} async-done(((bf16[2,320,4,640]{3,1,2,0:T(8,128)(2,1)}), bf16[2,1280,4,640]{3,1,2,0:T(8,128)(2,1)}) %all-gather.3.cloned.1.call-update) | async-done | bytes 13107216 | tf_op jit(solution)/shard_map/all_gather | solution.py:27
  270.7 6.2 %constant_dynamic-slice_fusion.2 = bf16[1,1280,4,640]{3,1,2,0:T(8,128)(2,1)} fusion(bf16[2,1280,4,640]{3,1,2,0:T(8,128)(2,1)} %all-gather.3.cloned.1.call-done, s32[]{:T(128)S(6)} %select_n.37), kind=kLoop, calls=%fused_computation.7 | loop fusion | bytes 13107204 | tf_op jit(solution)/shard_map/jit(dynamic_index_in_dim)/dynamic_slice | solution.py:28
  276.9 9.5 %copy.22 = bf16[1,1280,4,640]{1,3,2,0:T(8,128)(2,1)} copy(bf16[1,1280,4,640]{3,1,2,0:T(8,128)(2,1)} %constant_dynamic-slice_fusion.2) | data formatting | bytes 13107200 | tf_op jit(solution)/shard_map/jit(dynamic_index_in_dim)/dynamic_slice | solution.py:28
  286.4 14.6 %fusion.3 = f32[1280,1280]{1,0:T(8,128)} fusion(bf16[1280,2560]{0,1:T(8,128)(2,1)} %bitcast.25, bf16[2560,1280]{1,0:T(8,128)(2,1)} %bitcast.24), kind=kOutput, calls=%fused_computation.11 | convolution fusion | flops 8388608000 | bytes 19660800 | tf_op jit(solution)/shard_map/dot_general | solution.py:33
  301.0 0.6 copy-done.4
  301.7 0.6 dynamic-slice
  302.9 198.9 %all-reduce.3.cloned.1.call-done = f32[1280,1280]{1,0:T(8,128)} async-done(((f32[1280,1280]{1,0:T(8,128)}), f32[1280,1280]{1,0:T(8,128)}) %all-reduce.3.cloned.1.call-update) | async-done | bytes 6553616
  501.9 0.9 constant_dynamic-slice_fusion
  502.8 0.7 all_to_all.14
  503.5 0.4 copy.32
  503.9 1.5 reshape.22
  505.4 9.7 %all-to-all-start = ((f32[64,1,400]{2,1,0:T(1,128)}), f32[64,1,400]{2,1,0:T(1,128)S(1)}, u32[]{:S(2)}, u32[]{:S(2)}) async-start(f32[64,1,400]{2,1,0:T(1,128)} %reshape.22), calls=%async_computation | async-start | bytes 262144 | tf_op jit(solution)/shard_map/all_to_all | solution.py:37
  515.1 0.7 fusion.2
  517.1 9.1 %all-to-all-done = f32[64,1,400]{2,1,0:T(1,128)S(1)} async-done(((f32[64,1,400]{2,1,0:T(1,128)}), f32[64,1,400]{2,1,0:T(1,128)S(1)}, u32[]{:S(2)}, u32[]{:S(2)}) %all-to-all-start) | async-done | bytes 102432 | tf_op jit(solution)/shard_map/all_to_all | solution.py:37
  526.2 0.5 broadcast.7
  526.7 1.0 reduce
  527.7 0.3 reshape.23
  528.1 0.2 copy.28
  528.3 2.8 collective-permute-start
  531.1 0.1 dynamic-slice_subtract_fusion
  531.2 3.2 collective-permute-done
  534.4 1.0 fusion.1
  535.4 0.7 copy.27
  (18 shorter events, 0.2 us)
Async XLA Ops:
  6.5 6.2 %copy-start = (s32[2,5,4,10]{3,2,1,0:T(4,128)S(1)}, s32[2,5,4,10]{3,2,1,0:T(4,128)}, u32[]{:S(2)}) copy-start(s32[2,5,4,10]{3,2,1,0:T(4,128)} %param.8) | copy-start | bytes 4804
  6.5 135.7 %all-gather.5.cloned.1.call-start = ((), (), s32[]{:S(2)}) async-start(), calls=%async_computation.2 | async-start | bytes 16384000 | tf_op jit(solution)/shard_map/all_gather | solution.py:31
  12.7 258.0 %all-gather.3.cloned.1.call-start = ((), (), s32[]{:S(2)}) async-start(), calls=%async_computation.1 | async-start | bytes 16384000 | tf_op jit(solution)/shard_map/all_gather | solution.py:27
  29.9 5.1 copy-start.3
  34.7 467.2 %all-reduce.3.cloned.1.call-start = ((), (), s32[]{:S(2)}) async-start(), calls=%async_computation.3 | async-start | bytes 13107200
  301.0 0.7 copy-start.4
  301.0 214.1 %copy-start.2 = (f32[2]{0:T(128)S(1)}, f32[2]{0:T(128)}, u32[]{:S(2)}) copy-start(f32[2]{0:T(128)} %param.9) | copy-start | bytes 28
  301.0 230.1 %copy-start.1 = (f32[1280]{0:T(1024)S(1)}, f32[1280]{0:T(1024)}, u32[]{:S(2)}) copy-start(f32[1280]{0:T(1024)} %param.10) | copy-start | bytes 15364
  505.4 20.8 %all-to-all-start = ((f32[64,1,400]{2,1,0:T(1,128)}), f32[64,1,400]{2,1,0:T(1,128)S(1)}, u32[]{:S(2)}, u32[]{:S(2)}) async-start(f32[64,1,400]{2,1,0:T(1,128)} %reshape.22), calls=%async_computation | async-start | bytes 262144 | tf_op jit(solution)/shard_map/all_to_all | solution.py:37
  528.3 6.1 %collective-permute-start = (f32[1280,20]{0,1:T(8,128)S(1)}, f32[1280,20]{0,1:T(8,128)S(1)}, u32[]{:S(2)}, u32[]{:S(2)}) collective-permute-start(f32[1280,20]{0,1:T(8,128)S(1)} %copy.28), channel_id=1, source_target_pairs={{0,2},{1,3},{2,0},{3,1},{4,6},{5,7},{6,4},{7,5},{8,10},{9,11},{10,... | collective-permute-start | bytes 307208 | tf_op jit(solution)/shard_map/ppermute | solution.py:10
Sparse Core Ops, SparseCore 0:
  12.8 129.3 all-gather.4
  144.1 126.5 all-gather.2
  301.2 200.6 all-reduce.2
where the time goes:
time: 544 us; the launch traced here: 543 us
  waiting for transfers between devices  423 us (78%)
  local copies, waits for them, and re-layouts  67.3 us (12%)
  between operations  17.9 us (3%)
  matrix products  14.6 us (3%)
  starting transfers between devices  12.7 us (2%)
  other arithmetic  6.84 us (1%)
    unnamed x4, waiting for transfers between devices  199 us
    all_gather x1, waiting for transfers between devices, body(): gathered = lax.all_gather(masked, 'pair', axis=1, tiled=True)  108 us
    all_gather x1, waiting for transfers between devices, body(): segment = lax.all_gather(integrals, 'pair', axis=3, tiled=True)  104 us
    unnamed x16, local copies, waits for them, and re-layouts  22.7 us
    dynamic_slice x2, local copies, waits for them, and re-layouts, body(): lax.dynamic_index_in_dim(gathered, occ_first, 0, keepdims=False)  15.7 us
    dot_general x1, matrix products, body(): jnp.dot(left_block, picked.reshape(inner_size, segment.shape[3]), preferr...  14.6 us
    convert_element_type x2, local copies, waits for them, and re-layouts, body(): expanded.reshape(amplitudes.shape).astype(jnp.bfloat16)  11.7 us
  transfers between devices with their start and end apart: 5, of which 5 were waited for; matrix products, arithmetic and copies ran while one was open for 8% of the time, Pallas kernels for 0%

commit v1 on v0

v1 whole, which is shorter than its diff:
```python
import functools

import jax
import jax.numpy as jnp
from jax import lax
from jax.experimental import pallas as pl
from jax.experimental.pallas import tpu as pltpu
from jax.sharding import Mesh, PartitionSpec as P

AXES = ("zh", "zm", "zp", "x", "core", "y")
Z = ("zh", "zm", "zp")
ALL = ("zh", "zm", "zp", "x", "core")
F32 = jnp.float32


def permute(value, axis, target):
    return lax.ppermute(value, axis, [(s, target(s)) for s in range(lax.axis_size(axis))])


def prepare_kernel(chunks, mask_ref, rows_ref, out_ref):
    for n, t in enumerate(chunks):

        @pl.when(pl.program_id(0) == n)
        def _(t=t):
            for x in range(4):
                for core in range(2):
                    group = []
                    for i in range(2):
                        for zp in range(2):
                            tile = (zp * 160 + (x * 2 + core) * 20 + 4 * t) // 64
                            value = rows_ref[i, zp, x * 2 + core, 0] * mask_ref[i, tile][None]
                            group.append(value.astype(F32))
                    value = jnp.transpose(jnp.concatenate(group, 0), (1, 0, 2))
                    value = value.astype(jnp.bfloat16)
                    at = core * 64 + x * 16
                    for k in range(value.shape[0]):
                        out_ref[0, k, at : at + 16, :] = value[k]


def prepare(amplitudes, mask, lo, hi):
    return pl.pallas_call(
        functools.partial(prepare_kernel, tuple(range(lo, hi))),
        grid=(hi - lo,),
        out_shape=jax.ShapeDtypeStruct((hi - lo, 4, 128, 640), jnp.bfloat16),
        in_specs=[
            pl.BlockSpec((2, 5, 4, 640), lambda t: (0, 0, 0, 0)),
            pl.BlockSpec((2, 2, 8, 1, 4, 4, 640), lambda t: (0, 0, 0, t + lo, 0, 0, 0)),
        ],
        out_specs=pl.BlockSpec((1, 4, 128, 640), lambda t: (t, 0, 0, 0)),
        compiler_params=pltpu.CompilerParams(vmem_limit_bytes=40 * 2**20),
        cost_estimate=pl.CostEstimate(flops=1, bytes_accessed=1, transcendentals=0),
    )(mask, amplitudes.reshape(2, 2, 8, 5, 4, 4, 640))


def product_kernel(jobs, n_left, n_right, core_ref, *refs):
    left = refs[:n_left]
    right = refs[n_left : n_left + n_right]
    keep_ref, send_ref = refs[n_left + n_right :]
    me = core_ref[0]
    for li, ri, base in jobs:
        a_ref, b_ref = left[li], right[ri]
        chunks, depth = a_ref.shape[0], a_ref.shape[1]
        columns = b_ref.shape[1]
        for start in range(0, columns, 256):
            width = min(256, columns - start)
            acc = None
            for k in range(depth):
                part = lax.dot_general(
                    a_ref[:, k].reshape(chunks * 128, a_ref.shape[3]),
                    b_ref[k, start : start + width],
                    (((1,), (1,)), ((), ())),
                    preferred_element_type=F32,
                )
                acc = part if acc is None else acc + part
            acc = acc.reshape(chunks, 2, 4, 16, width)
            low, high = acc[:, 0], acc[:, 1]
            keep = jnp.where(me == 0, low, high)
            send = jnp.where(me == 0, high, low)
            for n in range(chunks):
                for c in range(width // 128):
                    at = base + n * (columns // 128) + start // 128 + c
                    span = slice(c * 128, (c + 1) * 128)
                    keep_ref[:, at] = keep[n, :, :, span]
                    send_ref[:, at] = send[n, :, :, span]


def product(core, left, right, pairs):
    jobs, base = [], 0
    for li, ri in pairs:
        jobs.append((li, ri, base))
        count = left[li].shape[0] * (right[ri].shape[1] // 128)
        base += count
    half = jax.ShapeDtypeStruct((4, base, 16, 128), F32)
    vmem = pl.BlockSpec(memory_space=pltpu.VMEM)
    return pl.pallas_call(
        functools.partial(product_kernel, jobs, len(left), len(right)),
        out_shape=(half, half),
        in_specs=[pl.BlockSpec(memory_space=pltpu.SMEM)] + [vmem] * (len(left) + len(right)),
        out_specs=(vmem, vmem),
        compiler_params=pltpu.CompilerParams(vmem_limit_bytes=40 * 2**20),
        cost_estimate=pl.CostEstimate(flops=1, bytes_accessed=1, transcendentals=0),
    )(core, *left, *right)


def reduce_chip(keep, send):
    got = permute(send, "core", lambda s: 1 - s)
    mine = place_on("x")
    spots = [mine, (mine + 1) & 3, (mine + 2) & 3, (mine + 3) & 3]
    return [take(keep, at) + take(got, at) for at in spots]


def reduce_x(parts):
    moved = [permute(parts[r], "x", lambda s, r=r: (s + r) % 4) for r in (1, 2, 3)]
    return parts[0] + moved[0] + moved[1] + moved[2]


def exchange_ring(parts, axis):
    moved = [parts[0]] + [permute(parts[r], axis, lambda s, r=r: (s + r) % 4) for r in (1, 2, 3)]
    ring = jnp.stack(moved[::-1] + moved[::-1])
    return lax.dynamic_slice_in_dim(ring, 3 - place_on(axis), 4)


def place_on(axis):
    return lax.axis_index(axis).astype(jnp.uint32)


def take(value, at):
    return lax.dynamic_index_in_dim(value, at, 0, keepdims=False)


def tie(first, second):
    return lax.optimization_barrier((first, second))[0]


def reduce_z(total):
    tiles = total.shape[0]
    value = total.reshape(tiles, 2, 2, 2, 2, 128)
    value = value.transpose(2, 4, 3, 0, 1, 5).reshape(2, 2, 2, tiles * 2, 128)
    for axis in Z[::-1]:
        mine = place_on(axis)
        keep, send = take(value, mine), take(value, 1 - mine)
        got = permute(send, axis, lambda s: 1 - s)
        value = keep + got if axis != Z[0] else None
    return keep, got


def assemble_kernel(places, *refs):
    out_ref = refs[-1]
    for n, place in enumerate(places):
        keep_ref, got_ref = refs[2 * n : 2 * n + 2]
        for m, (rs, rt, cs, ct) in enumerate(place):
            at = (cs * 5 + ct) * 128
            for i in range(2):
                row = slice(2 * m + i, 2 * m + i + 1)
                value = keep_ref[row, :] + got_ref[row, :]
                out_ref[i, rs * 5 + rt : rs * 5 + rt + 1, at : at + 128] = value


def assemble(places, pieces):
    flat = [v for pair in pieces for v in pair]
    vmem = pl.BlockSpec(memory_space=pltpu.VMEM)
    return pl.pallas_call(
        functools.partial(assemble_kernel, places),
        out_shape=jax.ShapeDtypeStruct((2, 10, 1280), F32),
        in_specs=[vmem] * len(flat),
        out_specs=vmem,
        cost_estimate=pl.CostEstimate(flops=1, bytes_accessed=1, transcendentals=0),
    )(*flat)


def body(amplitudes, integrals, screen, occ_energy, vir_energy, owner):
    core = lax.axis_index("core").astype(jnp.int32).reshape(1)
    mask = jnp.repeat(screen, 64, axis=3).astype(jnp.bfloat16)

    own_right = integrals.transpose(0, 2, 3, 1).reshape(4, 640, 640)
    far_right = permute(own_right, "y", lambda s: 3 - s)
    own_left = prepare(amplitudes, mask, 0, 5)
    far_left = permute(own_left, "y", lambda s: s ^ 1)

    def cells_of(row_source, col_source):
        return [(row_source, r, col_source, c) for r in range(5) for c in range(5)]

    def block(left, right):
        pairs = [(l, r) for l in range(len(left)) for r in range(len(right))]
        keep, send = product(core, left, right, pairs)
        return keep, reduce_chip(keep, send)

    total = reduce_x(block([own_left], [own_right])[1])
    pieces = [reduce_z(total)]
    far_right = tie(far_right, pieces[0][0])
    keep, parts_a = block([own_left], [far_right])
    total_a = reduce_x(parts_a)
    far_left = tie(far_left, keep)
    total_b = reduce_x(block([far_left], [own_right, far_right])[1])
    pieces.append(reduce_z(jnp.concatenate([total_a, total_b])))
    places = [cells_of(0, 0), cells_of(0, 1) + cells_of(1, 0) + cells_of(1, 1)]
    full = assemble(places, pieces)
    full = full.reshape(2, 10, 2, 2, 320)

    turn = (lax.axis_index("y") + jnp.arange(4)) & 3
    combo = jnp.sum(jnp.where(turn[:, None] == jnp.arange(4)[None], owner[None], 0), axis=1)
    wanted = jnp.stack([combo, 2 * (combo & 1) + (combo >> 1)], axis=1)[:, :, None, None]
    by_pair = [full[i, :, :, j].reshape(10, 640) for i in range(2) for j in range(2)]
    got = jnp.where(
        wanted < 2,
        jnp.where(wanted == 0, by_pair[0], by_pair[1]),
        jnp.where(wanted == 2, by_pair[2], by_pair[3]),
    ).reshape(4, 20, 640)
    got = exchange_ring(got, "y").reshape(4, 2, 2, 5, 2, 320)
    cells = (
        ((0, 0), (1, 0), (1, 1), (0, 1)),
        ((3, 1), (2, 1), (2, 0), (3, 0)),
    )
    rows = []
    for q in range(4):
        cols = [
            got[source, :, 0 if source == q else 1, :, side] for source, side in cells[q // 2]
        ]
        rows.append(jnp.concatenate(cols, axis=-1))
    rows = jnp.stack(rows, axis=1)
    swapped = rows[1].reshape(20, 1280)
    swapped = swapped.reshape(20, 64, 20).transpose(1, 0, 2).reshape(64, 400)
    home, swapped = lax.optimization_barrier((rows[0], swapped))
    mirrored = lax.all_to_all(swapped, ALL, split_axis=0, concat_axis=0, tiled=True)
    mirrored = mirrored.reshape(4, 2, 8, 4, 5, 20).transpose(5, 3, 1, 2, 4, 0).reshape(20, 1280)
    me = place_on(("zh", "zm"))
    direct = exchange_ring([take(home, (me + r) & 3) for r in range(4)], ("zh", "zm"))
    direct = direct.transpose(1, 0, 2).reshape(20, 1280)

    mine = combo[:1]
    first = jnp.where(mine < 2, occ_energy[:1], occ_energy[1:])
    second = jnp.where((mine & 1) == 0, occ_energy[:1], occ_energy[1:])
    row_energy = lax.dynamic_slice_in_dim(vir_energy, place_on(ALL) * 20, 20)
    gap = (first + second)[:, None] - row_energy[:, None] - vir_energy[None, :]
    return ((direct + mirrored) / gap)[None]


def solution(mesh):
    fine = Mesh(mesh.devices.reshape(2, 2, 2, 4, 2, 4), AXES)
    vir = ("zm", "zp", "x", "core")
    return jax.shard_map(
        body,
        mesh=fine,
        in_specs=(
            P(None, "y", vir, "zh"),
            P(vir, "zh", None, "y"),
            P(None, "y", vir, "zh"),
            P(),
            P(),
            P(),
        ),
        out_specs=P("y", ALL, None),
        check_vma=False,
    )
```

time: 544 us -> 207 us (0.38)
  waiting for transfers between devices: 423 us -> 91 us
  starting transfers between devices: 12.7 us -> 66.6 us
  local copies, waits for them, and re-layouts: 67.3 us -> 17.6 us
  Pallas kernels: 0 us -> 22 us
  between operations: 17.9 us -> 3.19 us
  matrix products: 14.6 us -> 0 us
    all_gather x2 -> x0, waiting for transfers between devices: 212 us -> none  [the longest x1 108 us: body(): gathered = lax.all_gather(masked, 'pair', axis=1, tiled=True)]
    unnamed x4 -> x0, waiting for transfers between devices: 199 us -> none
    ppermute x1 -> x26, waiting for transfers between devices: 3.2 us -> 80.4 us  [permute(): lax.ppermute(value, axis, [(s, target(s)) for s in range(lax.axis_size(ax...]
    ppermute x1 -> x26, starting transfers between devices: 2.8 us -> 53.7 us  [permute(): lax.ppermute(value, axis, [(s, target(s)) for s in range(lax.axis_size(ax...]
    dynamic_slice x5 -> x6, local copies, waits for them, and re-layouts: 24.8 us -> 1.07 us  [the longest x5 1.04 us: take(): return lax.dynamic_index_in_dim(value, at, 0, keepdims=False)]
    pallas_call x0 -> x5, Pallas kernels: none -> 22 us  [the longest x3 18.1 us: product(): pl.pallas_call(functools.partial(product_kernel, jobs, len(left), len(rig...]
    unnamed x16 -> x31, local copies, waits for them, and re-layouts: 22.7 us -> 6.4 us
    dot_general x1 -> x0, matrix products: 14.6 us -> none  [body(): jnp.dot(left_block, picked.reshape(inner_size, segment.shape[3]), preferr...]
  transfers between devices with their start and end apart: 5 -> 27, of which waited for: 5 -> 20; matrix products, arithmetic and copies ran while one was open for 8% -> 5% of each run, Pallas kernels for 0% -> 6%
where the time goes in v1:
time: 207 us
  waiting for transfers between devices  91 us (44%)
  starting transfers between devices  66.6 us (32%)
  Pallas kernels  22 us (11%)
  local copies, waits for them, and re-layouts  17.6 us (9%)
  other arithmetic  6.66 us (3%)
  between operations  3.19 us (2%)
    ppermute x26, waiting for transfers between devices, permute(): lax.ppermute(value, axis, [(s, target(s)) for s in range(lax.axis_size(ax...  80.4 us
    ppermute x26, starting transfers between devices, permute(): lax.ppermute(value, axis, [(s, target(s)) for s in range(lax.axis_size(ax...  53.7 us
    pallas_call x3, Pallas kernels, product(): pl.pallas_call(functools.partial(product_kernel, jobs, len(left), len(rig...  18.1 us
    all_to_all x1, starting transfers between devices, body(): lax.all_to_all(swapped, ALL, split_axis=0, concat_axis=0, tiled=True)  12.8 us
    all_to_all x1, waiting for transfers between devices, body(): lax.all_to_all(swapped, ALL, split_axis=0, concat_axis=0, tiled=True)  10.6 us
    unnamed x31, local copies, waits for them, and re-layouts  6.4 us
  transfers between devices with their start and end apart: 27, of which 20 were waited for; matrix products, arithmetic and copies ran while one was open for 5% of the time, Pallas kernels for 6%

profile of v1, /device:TPU:1, one launch (start us, length us, event | category | flops | bytes accessed | tf_op | source)
XLA Modules:
  0.0 207.1 jit_solution(3946624537496890872)
XLA Ops:
  0.0 3.6 %collective-permute-start.7 = (bf16[4,640,640]{2,1,0:T(8,128)(2,1)}, bf16[4,640,640]{2,1,0:T(8,128)(2,1)}, u32[]{:S(2)}, u32[]{:S(2)}) collective-permute-start(bf16[4,640,640]{2,1,0:T(8,128)(2,1)} %bitcast.195), channel_id=1, source_target_pairs={{0,3},{1,2},{2,1},{3,0},{4,7},{5,6},{6,5},{7,4},{8,11},{9,10},{10,... | collective-permute-start | bytes 9830408 | tf_op jit(solution)/shard_map/ppermute | solution.py:17
  6.5 2.2 %shard_map.64.refs_0_ = bf16[5,4,128,640]{3,2,1,0:T(8,128)(2,1)S(1)} custom-call(bf16[2,5,4,640]{3,2,1,0:T(4,128)(2,1)S(1)} %convert_element_type.33.mask_ref, bf16[2,2,8,5,4,4,640]{6,5,4,3,2,1,0:T(4,128)(2,1)S(1)} %bitcast.198), custom_call_target="tpu_custom_call" | custom-call | flops 1 | bytes 1 | tf_op jit(solution)/shard_map/pallas_call | solution.py:41
  10.8 4.1 %shard_map.65 = (f32[4,25,16,128]{3,2,1,0:T(8,128)S(1)}, f32[4,25,16,128]{3,2,1,0:T(8,128)}) custom-call(s32[1]{0:T(128)} %bitcast.1.core_ref, bf16[5,4,128,640]{3,2,1,0:T(8,128)(2,1)S(1)} %shard_map.64.refs_0_, bf16[4,640,640]{2,1,0:T(8,128)(2,1)S(1)} %bitcast.196), custom_call_target="tpu_custom_call" | custom-call | flops 1 | bytes 1 | tf_op jit(solution)/shard_map/pallas_call | solution.py:95
  16.9 2.3 %collective-permute-done = f32[4,25,16,128]{3,2,1,0:T(8,128)} collective-permute-done((f32[4,25,16,128]{3,2,1,0:T(8,128)}, f32[4,25,16,128]{3,2,1,0:T(8,128)}, u32[]{:S(2)}, u32[]{:S(2)}) %collective-permute-start) | collective-permute-done | bytes 819232 | tf_op jit(solution)/shard_map/ppermute | solution.py:17
  19.2 2.2 %add_bitcast_fusion.8 = (f32[25,16,128]{2,1,0:T(8,128)}, f32[25,16,128]{2,1,0:T(8,128)}, f32[25,16,128]{2,1,0:T(8,128)}) fusion(f32[4,25,16,128]{3,2,1,0:T(8,128)} %collective-permute-done, u32[]{:T(128)S(6)} %and.59, f32[4,25,16,128]{3,2,1,0:T(8,128)} %copy-done.3, u32[]{:T(128)S(6)} %and.61, u32[]{:T(128)S(6)} %and.60), kind=kLoop, calls=%fused_computation.22 | loop fusion | flops 153600 | bytes 1843212 | tf_op jit(solution)/shard_map/add | solution.py:109
  22.7 2.4 %collective-permute-start.2 = (f32[25,16,128]{2,1,0:T(8,128)}, f32[25,16,128]{2,1,0:T(8,128)}, u32[]{:S(2)}, u32[]{:S(2)}) collective-permute-start(f32[25,16,128]{2,1,0:T(8,128)} %get-tuple-element.40), channel_id=1, source_target_pairs={{0,16},{8,24},{16,0},{24,8},{1,17},{9,25},{17,1},{25,9},{2,18},{10... | collective-permute-start | bytes 614408 | tf_op jit(solution)/shard_map/ppermute | solution.py:17
  26.3 3.0 %collective-permute-done.1 = f32[25,16,128]{2,1,0:T(8,128)S(1)} collective-permute-done((f32[25,16,128]{2,1,0:T(8,128)}, f32[25,16,128]{2,1,0:T(8,128)S(1)}, u32[]{:S(2)}, u32[]{:S(2)}) %collective-permute-start.1) | collective-permute-done | bytes 204832 | tf_op jit(solution)/shard_map/ppermute | solution.py:17
  29.3 5.4 %collective-permute-done.2 = f32[25,16,128]{2,1,0:T(8,128)} collective-permute-done((f32[25,16,128]{2,1,0:T(8,128)}, f32[25,16,128]{2,1,0:T(8,128)}, u32[]{:S(2)}, u32[]{:S(2)}) %collective-permute-start.2) | collective-permute-done | bytes 204832 | tf_op jit(solution)/shard_map/ppermute | solution.py:17
  38.3 2.8 %collective-permute-done.4 = f32[2,2,50,128]{3,2,1,0:T(8,128)S(1)} collective-permute-done((f32[2,2,50,128]{3,2,1,0:T(8,128)}, f32[2,2,50,128]{3,2,1,0:T(8,128)S(1)}, u32[]{:S(2)}, u32[]{:S(2)}) %collective-permute-start.4) | collective-permute-done | bytes 102432 | tf_op jit(solution)/shard_map/ppermute | solution.py:17
  42.7 3.3 %collective-permute-start.5 = (f32[2,50,128]{2,1,0:T(8,128)S(1)}, f32[2,50,128]{2,1,0:T(8,128)S(1)}, u32[]{:S(2)}, u32[]{:S(2)}) collective-permute-start(f32[2,50,128]{2,1,0:T(8,128)S(1)} %dynamic-slice_bitcast_fusion.4), channel_id=1, source_target_pairs={{0,64},{64,0},{1,65},{65,1},{2,66},{66,2},{3,67},{67,3},{4,68},{68... | collective-permute-start | bytes 153608 | tf_op jit(solution)/shard_map/ppermute | solution.py:17
  45.9 2.0 collective-permute-done.5
  48.5 24.9 %collective-permute-done.7.refs_1_.refs_2_ = bf16[4,640,640]{2,1,0:T(8,128)(2,1)} collective-permute-done((bf16[4,640,640]{2,1,0:T(8,128)(2,1)}, bf16[4,640,640]{2,1,0:T(8,128)(2,1)}, u32[]{:S(2)}, u32[]{:S(2)}) %collective-permute-start.7) | collective-permute-done | bytes 3276832 | tf_op jit(solution)/shard_map/ppermute | solution.py:17
  73.5 5.1 %shard_map.66 = (f32[4,25,16,128]{3,2,1,0:T(8,128)S(1)}, f32[4,25,16,128]{3,2,1,0:T(8,128)S(1)}) custom-call(s32[1]{0:T(128)} %bitcast.1.core_ref, bf16[5,4,128,640]{3,2,1,0:T(8,128)(2,1)S(1)} %shard_map.64.refs_0_, bf16[4,640,640]{2,1,0:T(8,128)(2,1)} %collective-permute-done.7.refs_1_.refs_2_), custom_call_target="tpu_custom_call" | custom-call | flops 1 | bytes 1 | tf_op jit(solution)/shard_map/pallas_call | solution.py:95
  80.4 8.9 %shard_map.67 = (f32[4,50,16,128]{3,2,1,0:T(8,128)S(1)}, f32[4,50,16,128]{3,2,1,0:T(8,128)S(1)}) custom-call(s32[1]{0:T(128)} %bitcast.1.core_ref, bf16[5,4,128,640]{3,2,1,0:T(8,128)(2,1)} %collective-permute-done.12.refs_0_, bf16[4,640,640]{2,1,0:T(8,128)(2,1)S(1)} %bitcast.197, bf16[4,640,640]{2,1,0:T(8,128)(2,1)} %collective-permute-done.7.refs_1_.refs_2_), custom_call_target="tpu_custom_call" | custom-call | flops 1 | bytes 1 | tf_op jit(solution)/shard_map/pallas_call | solution.py:95
  91.4 4.2 %collective-permute-done.8 = f32[4,25,16,128]{3,2,1,0:T(8,128)S(1)} collective-permute-done((f32[4,25,16,128]{3,2,1,0:T(8,128)S(1)}, f32[4,25,16,128]{3,2,1,0:T(8,128)S(1)}, u32[]{:S(2)}, u32[]{:S(2)}) %collective-permute-start.8) | collective-permute-done | bytes 819232 | tf_op jit(solution)/shard_map/ppermute | solution.py:17
  95.6 2.8 %collective-permute-start.10 = (f32[25,16,128]{2,1,0:T(8,128)S(1)}, f32[25,16,128]{2,1,0:T(8,128)S(1)}, u32[]{:S(2)}, u32[]{:S(2)}) collective-permute-start(f32[25,16,128]{2,1,0:T(8,128)S(1)} %get-tuple-element.37), channel_id=1, source_target_pairs={{0,16},{8,24},{16,0},{24,8},{1,17},{9,25},{17,1},{25,9},{2,18},{10... | collective-permute-start | bytes 614408 | tf_op jit(solution)/shard_map/ppermute | solution.py:17
  100.5 2.9 %collective-permute-start.15 = (f32[50,16,128]{2,1,0:T(8,128)S(1)}, f32[50,16,128]{2,1,0:T(8,128)S(1)}, u32[]{:S(2)}, u32[]{:S(2)}) collective-permute-start(f32[50,16,128]{2,1,0:T(8,128)S(1)} %get-tuple-element.34), channel_id=1, source_target_pairs={{0,16},{8,24},{16,0},{24,8},{1,17},{9,25},{17,1},{25,9},{2,18},{10... | collective-permute-start | bytes 1228808 | tf_op jit(solution)/shard_map/ppermute | solution.py:17
  103.5 2.5 %collective-permute-start.16 = (f32[50,16,128]{2,1,0:T(8,128)S(1)}, f32[50,16,128]{2,1,0:T(8,128)S(1)}, u32[]{:S(2)}, u32[]{:S(2)}) collective-permute-start(f32[50,16,128]{2,1,0:T(8,128)S(1)} %get-tuple-element.33), channel_id=1, source_target_pairs={{0,24},{8,0},{16,8},{24,16},{1,25},{9,1},{17,9},{25,17},{2,26},{10... | collective-permute-start | bytes 1228808 | tf_op jit(solution)/shard_map/ppermute | solution.py:17
  106.0 2.0 collective-permute-done.11
  108.2 8.9 %collective-permute-done.14 = f32[50,16,128]{2,1,0:T(8,128)S(1)} collective-permute-done((f32[50,16,128]{2,1,0:T(8,128)S(1)}, f32[50,16,128]{2,1,0:T(8,128)S(1)}, u32[]{:S(2)}, u32[]{:S(2)}) %collective-permute-start.14) | collective-permute-done | bytes 409632 | tf_op jit(solution)/shard_map/ppermute | solution.py:17
  117.1 8.4 %collective-permute-done.15 = f32[50,16,128]{2,1,0:T(8,128)S(1)} collective-permute-done((f32[50,16,128]{2,1,0:T(8,128)S(1)}, f32[50,16,128]{2,1,0:T(8,128)S(1)}, u32[]{:S(2)}, u32[]{:S(2)}) %collective-permute-start.15) | collective-permute-done | bytes 409632 | tf_op jit(solution)/shard_map/ppermute | solution.py:17
  128.2 6.2 %collective-permute-done.17 = f32[2,2,150,128]{3,2,1,0:T(8,128)S(1)} collective-permute-done((f32[2,2,150,128]{3,2,1,0:T(8,128)S(1)}, f32[2,2,150,128]{3,2,1,0:T(8,128)S(1)}, u32[]{:S(2)}, u32[]{:S(2)}) %collective-permute-start.17) | collective-permute-done | bytes 307232 | tf_op jit(solution)/shard_map/ppermute | solution.py:17
  134.5 3.1 %collective-permute-start.18 = (f32[2,150,128]{2,1,0:T(8,128)S(1)}, f32[2,150,128]{2,1,0:T(8,128)S(1)}, u32[]{:S(2)}, u32[]{:S(2)}) collective-permute-start(f32[2,150,128]{2,1,0:T(8,128)S(1)} %dynamic-slice_bitcast_fusion), channel_id=1, source_target_pairs={{0,64},{64,0},{1,65},{65,1},{2,66},{66,2},{3,67},{67,3},{4,68},{68... | collective-permute-start | bytes 460808 | tf_op jit(solution)/shard_map/ppermute | solution.py:17
  137.6 4.8 %collective-permute-start.6 = (f32[50,128]{1,0:T(8,128)S(1)}, f32[50,128]{1,0:T(8,128)S(1)}, u32[]{:S(2)}, u32[]{:S(2)}) collective-permute-start(f32[50,128]{1,0:T(8,128)S(1)} %get-tuple-element.70), channel_id=1, source_target_pairs={{0,128},{128,0},{1,129},{129,1},{2,130},{130,2},{3,131},{131,3},{4... | collective-permute-start | bytes 76808 | tf_op jit(solution)/shard_map/ppermute | solution.py:17
  142.3 2.0 collective-permute-done.18
  145.0 7.3 %collective-permute-start.19 = (f32[150,128]{1,0:T(8,128)S(1)}, f32[150,128]{1,0:T(8,128)S(1)}, u32[]{:S(2)}, u32[]{:S(2)}) collective-permute-start(f32[150,128]{1,0:T(8,128)S(1)} %get-tuple-element.64), channel_id=1, source_target_pairs={{0,128},{128,0},{1,129},{129,1},{2,130},{130,2},{3,131},{131,3},{4... | collective-permute-start | bytes 230408 | tf_op jit(solution)/shard_map/ppermute | solution.py:17
  164.3 3.9 %collective-permute-done.21 = f32[20,640]{1,0:T(8,128)S(1)} collective-permute-done((f32[20,640]{1,0:T(8,128)S(1)}, f32[20,640]{1,0:T(8,128)S(1)}, u32[]{:S(2)}, u32[]{:S(2)}) %collective-permute-start.21) | collective-permute-done | bytes 51232 | tf_op jit(solution)/shard_map/ppermute | solution.py:17
  171.8 2.6 %collective-permute-start.23 = (f32[5,1280]{1,0:T(8,128)S(1)}, f32[5,1280]{1,0:T(8,128)S(1)}, u32[]{:S(2)}, u32[]{:S(2)}) collective-permute-start(f32[5,1280]{1,0:T(8,128)S(1)} %bitcast.213), channel_id=1, source_target_pairs={{0,192},{64,0},{128,64},{192,128},{1,193},{65,1},{129,65},{193,129... | collective-permute-start | bytes 76808 | tf_op jit(solution)/shard_map/ppermute | solution.py:17
  174.4 2.9 %collective-permute-start.24 = (f32[5,1280]{1,0:T(8,128)S(1)}, f32[5,1280]{1,0:T(8,128)S(1)}, u32[]{:S(2)}, u32[]{:S(2)}) collective-permute-start(f32[5,1280]{1,0:T(8,128)S(1)} %bitcast.214), channel_id=1, source_target_pairs={{0,128},{64,192},{128,0},{192,64},{1,129},{65,193},{129,1},{193,65... | collective-permute-start | bytes 76808 | tf_op jit(solution)/shard_map/ppermute | solution.py:17
  177.4 2.3 %collective-permute-start.25 = (f32[5,1280]{1,0:T(8,128)S(1)}, f32[5,1280]{1,0:T(8,128)S(1)}, u32[]{:S(2)}, u32[]{:S(2)}) collective-permute-start(f32[5,1280]{1,0:T(8,128)S(1)} %bitcast.215), channel_id=1, source_target_pairs={{0,64},{64,128},{128,192},{192,0},{1,65},{65,129},{129,193},{193,1... | collective-permute-start | bytes 76808 | tf_op jit(solution)/shard_map/ppermute | solution.py:17
  180.5 12.8 %all-to-all-start = ((f32[64,1,400]{2,1,0:T(1,128)}), f32[64,1,400]{2,1,0:T(1,128)S(1)}, u32[]{:S(2)}, u32[]{:S(2)}) async-start(f32[64,1,400]{2,1,0:T(1,128)} %copy.563), calls=%async_computation | async-start | bytes 262144 | tf_op jit(solution)/shard_map/all_to_all | solution.py:224
  193.8 10.6 %all-to-all-done = f32[64,1,400]{2,1,0:T(1,128)S(1)} async-done(((f32[64,1,400]{2,1,0:T(1,128)}), f32[64,1,400]{2,1,0:T(1,128)S(1)}, u32[]{:S(2)}, u32[]{:S(2)}) %all-to-all-start) | async-done | bytes 102432 | tf_op jit(solution)/shard_map/all_to_all | solution.py:224
  (132 shorter events, 41.4 us)
Async XLA Ops:
  0.0 73.5 %collective-permute-start.7 = (bf16[4,640,640]{2,1,0:T(8,128)(2,1)}, bf16[4,640,640]{2,1,0:T(8,128)(2,1)}, u32[]{:S(2)}, u32[]{:S(2)}) collective-permute-start(bf16[4,640,640]{2,1,0:T(8,128)(2,1)} %bitcast.195), channel_id=1, source_target_pairs={{0,3},{1,2},{2,1},{3,0},{4,7},{5,6},{6,5},{7,4},{8,11},{9,10},{10,... | collective-permute-start | bytes 9830408 | tf_op jit(solution)/shard_map/ppermute | solution.py:17
  4.6 1.9 copy-start.2
  8.8 71.7 %collective-permute-start.12 = (bf16[5,4,128,640]{3,2,1,0:T(8,128)(2,1)S(1)}, bf16[5,4,128,640]{3,2,1,0:T(8,128)(2,1)}, u32[]{:S(2)}, u32[]{:S(2)}) collective-permute-start(bf16[5,4,128,640]{3,2,1,0:T(8,128)(2,1)S(1)} %shard_map.64.refs_0_), channel_id=1, source_target_pairs={{0,1},{1,0},{2,3},{3,2},{4,5},{5,4},{6,7},{7,6},{8,9},{9,8},{10,11... | collective-permute-start | bytes 9830408 | tf_op jit(solution)/shard_map/ppermute | solution.py:17
  15.8 3.4 %collective-permute-start = (f32[4,25,16,128]{3,2,1,0:T(8,128)}, f32[4,25,16,128]{3,2,1,0:T(8,128)}, u32[]{:S(2)}, u32[]{:S(2)}) collective-permute-start(f32[4,25,16,128]{3,2,1,0:T(8,128)} %get-tuple-element.16), channel_id=1, source_target_pairs={{0,4},{4,0},{1,5},{5,1},{2,6},{6,2},{3,7},{7,3},{8,12},{12,8},{9,1... | collective-permute-start | bytes 2457608 | tf_op jit(solution)/shard_map/ppermute | solution.py:17
  21.4 7.8 %collective-permute-start.1 = (f32[25,16,128]{2,1,0:T(8,128)}, f32[25,16,128]{2,1,0:T(8,128)S(1)}, u32[]{:S(2)}, u32[]{:S(2)}) collective-permute-start(f32[25,16,128]{2,1,0:T(8,128)} %get-tuple-element.38), channel_id=1, source_target_pairs={{0,8},{8,16},{16,24},{24,0},{1,9},{9,17},{17,25},{25,1},{2,10},{10... | collective-permute-start | bytes 614408 | tf_op jit(solution)/shard_map/ppermute | solution.py:17
  22.7 12.0 %collective-permute-start.2 = (f32[25,16,128]{2,1,0:T(8,128)}, f32[25,16,128]{2,1,0:T(8,128)}, u32[]{:S(2)}, u32[]{:S(2)}) collective-permute-start(f32[25,16,128]{2,1,0:T(8,128)} %get-tuple-element.40), channel_id=1, source_target_pairs={{0,16},{8,24},{16,0},{24,8},{1,17},{9,25},{17,1},{25,9},{2,18},{10... | collective-permute-start | bytes 614408 | tf_op jit(solution)/shard_map/ppermute | solution.py:17
  25.1 9.5 %collective-permute-start.3 = (f32[25,16,128]{2,1,0:T(8,128)}, f32[25,16,128]{2,1,0:T(8,128)}, u32[]{:S(2)}, u32[]{:S(2)}) collective-permute-start(f32[25,16,128]{2,1,0:T(8,128)} %get-tuple-element.39), channel_id=1, source_target_pairs={{0,24},{8,0},{16,8},{24,16},{1,25},{9,1},{17,9},{25,17},{2,26},{10... | collective-permute-start | bytes 614408 | tf_op jit(solution)/shard_map/ppermute | solution.py:17
  36.7 4.4 %collective-permute-start.4 = (f32[2,2,50,128]{3,2,1,0:T(8,128)}, f32[2,2,50,128]{3,2,1,0:T(8,128)S(1)}, u32[]{:S(2)}, u32[]{:S(2)}) collective-permute-start(f32[2,2,50,128]{3,2,1,0:T(8,128)} %bitcast.189), channel_id=1, source_target_pairs={{0,32},{32,0},{1,33},{33,1},{2,34},{34,2},{3,35},{35,3},{4,36},{36... | collective-permute-start | bytes 307208 | tf_op jit(solution)/shard_map/ppermute | solution.py:17
  42.7 5.2 %collective-permute-start.5 = (f32[2,50,128]{2,1,0:T(8,128)S(1)}, f32[2,50,128]{2,1,0:T(8,128)S(1)}, u32[]{:S(2)}, u32[]{:S(2)}) collective-permute-start(f32[2,50,128]{2,1,0:T(8,128)S(1)} %dynamic-slice_bitcast_fusion.4), channel_id=1, source_target_pairs={{0,64},{64,0},{1,65},{65,1},{2,66},{66,2},{3,67},{67,3},{4,68},{68... | collective-permute-start | bytes 153608 | tf_op jit(solution)/shard_map/ppermute | solution.py:17
  73.5 7.0 %copy-start.1 = (bf16[4,640,2,320]{1,3,2,0:T(8,128)(2,1)S(1)}, bf16[4,640,2,320]{1,3,2,0:T(8,128)(2,1)}, u32[]{:S(2)}) copy-start(bf16[4,640,2,320]{1,3,2,0:T(8,128)(2,1)} %param.7) | copy-start | bytes 9830404
  89.3 10.6 %collective-permute-start.13 = (f32[4,50,16,128]{3,2,1,0:T(8,128)S(1)}, f32[4,50,16,128]{3,2,1,0:T(8,128)S(1)}, u32[]{:S(2)}, u32[]{:S(2)}) collective-permute-start(f32[4,50,16,128]{3,2,1,0:T(8,128)S(1)} %get-tuple-element.22), channel_id=1, source_target_pairs={{0,4},{4,0},{1,5},{5,1},{2,6},{6,2},{3,7},{7,3},{8,12},{12,8},{9,1... | collective-permute-start | bytes 4915208 | tf_op jit(solution)/shard_map/ppermute | solution.py:17
  91.3 4.3 %collective-permute-start.8 = (f32[4,25,16,128]{3,2,1,0:T(8,128)S(1)}, f32[4,25,16,128]{3,2,1,0:T(8,128)S(1)}, u32[]{:S(2)}, u32[]{:S(2)}) collective-permute-start(f32[4,25,16,128]{3,2,1,0:T(8,128)S(1)} %get-tuple-element.19), channel_id=1, source_target_pairs={{0,4},{4,0},{1,5},{5,1},{2,6},{6,2},{3,7},{7,3},{8,12},{12,8},{9,1... | collective-permute-start | bytes 2457608 | tf_op jit(solution)/shard_map/ppermute | solution.py:17
  95.6 7.9 %collective-permute-start.10 = (f32[25,16,128]{2,1,0:T(8,128)S(1)}, f32[25,16,128]{2,1,0:T(8,128)S(1)}, u32[]{:S(2)}, u32[]{:S(2)}) collective-permute-start(f32[25,16,128]{2,1,0:T(8,128)S(1)} %get-tuple-element.37), channel_id=1, source_target_pairs={{0,16},{8,24},{16,0},{24,8},{1,17},{9,25},{17,1},{25,9},{2,18},{10... | collective-permute-start | bytes 614408 | tf_op jit(solution)/shard_map/ppermute | solution.py:17
  98.5 9.6 %collective-permute-start.11 = (f32[25,16,128]{2,1,0:T(8,128)S(1)}, f32[25,16,128]{2,1,0:T(8,128)S(1)}, u32[]{:S(2)}, u32[]{:S(2)}) collective-permute-start(f32[25,16,128]{2,1,0:T(8,128)S(1)} %get-tuple-element.36), channel_id=1, source_target_pairs={{0,24},{8,0},{16,8},{24,16},{1,25},{9,1},{17,9},{25,17},{2,26},{10... | collective-permute-start | bytes 614408 | tf_op jit(solution)/shard_map/ppermute | solution.py:17
  99.3 8.8 %collective-permute-start.9 = (f32[25,16,128]{2,1,0:T(8,128)S(1)}, f32[25,16,128]{2,1,0:T(8,128)S(1)}, u32[]{:S(2)}, u32[]{:S(2)}) collective-permute-start(f32[25,16,128]{2,1,0:T(8,128)S(1)} %get-tuple-element.35), channel_id=1, source_target_pairs={{0,8},{8,16},{16,24},{24,0},{1,9},{9,17},{17,25},{25,1},{2,10},{10... | collective-permute-start | bytes 614408 | tf_op jit(solution)/shard_map/ppermute | solution.py:17
  100.1 17.0 %collective-permute-start.14 = (f32[50,16,128]{2,1,0:T(8,128)S(1)}, f32[50,16,128]{2,1,0:T(8,128)S(1)}, u32[]{:S(2)}, u32[]{:S(2)}) collective-permute-start(f32[50,16,128]{2,1,0:T(8,128)S(1)} %get-tuple-element.32), channel_id=1, source_target_pairs={{0,8},{8,16},{16,24},{24,0},{1,9},{9,17},{17,25},{25,1},{2,10},{10... | collective-permute-start | bytes 1228808 | tf_op jit(solution)/shard_map/ppermute | solution.py:17
  100.5 25.0 %collective-permute-start.15 = (f32[50,16,128]{2,1,0:T(8,128)S(1)}, f32[50,16,128]{2,1,0:T(8,128)S(1)}, u32[]{:S(2)}, u32[]{:S(2)}) collective-permute-start(f32[50,16,128]{2,1,0:T(8,128)S(1)} %get-tuple-element.34), channel_id=1, source_target_pairs={{0,16},{8,24},{16,0},{24,8},{1,17},{9,25},{17,1},{25,9},{2,18},{10... | collective-permute-start | bytes 1228808 | tf_op jit(solution)/shard_map/ppermute | solution.py:17
  103.5 22.1 %collective-permute-start.16 = (f32[50,16,128]{2,1,0:T(8,128)S(1)}, f32[50,16,128]{2,1,0:T(8,128)S(1)}, u32[]{:S(2)}, u32[]{:S(2)}) collective-permute-start(f32[50,16,128]{2,1,0:T(8,128)S(1)} %get-tuple-element.33), channel_id=1, source_target_pairs={{0,24},{8,0},{16,8},{24,16},{1,25},{9,1},{17,9},{25,17},{2,26},{10... | collective-permute-start | bytes 1228808 | tf_op jit(solution)/shard_map/ppermute | solution.py:17
  125.8 2.3 %copy-start.9 = (s32[4]{0:T(128)S(1)}, s32[4]{0:T(128)}, u32[]{:S(2)}) copy-start(s32[4]{0:T(128)} %param.11) | copy-start | bytes 52
  126.1 8.3 %collective-permute-start.17 = (f32[2,2,150,128]{3,2,1,0:T(8,128)S(1)}, f32[2,2,150,128]{3,2,1,0:T(8,128)S(1)}, u32[]{:S(2)}, u32[]{:S(2)}) collective-permute-start(f32[2,2,150,128]{3,2,1,0:T(8,128)S(1)} %bitcast.208), channel_id=1, source_target_pairs={{0,32},{32,0},{1,33},{33,1},{2,34},{34,2},{3,35},{35,3},{4,36},{36... | collective-permute-start | bytes 921608 | tf_op jit(solution)/shard_map/ppermute | solution.py:17
  134.4 25.8 %copy-start.8 = (f32[2]{0:T(128)S(1)}, f32[2]{0:T(128)}, u32[]{:S(2)}) copy-start(f32[2]{0:T(128)} %param.9) | copy-start | bytes 28
  134.5 9.8 %collective-permute-start.18 = (f32[2,150,128]{2,1,0:T(8,128)S(1)}, f32[2,150,128]{2,1,0:T(8,128)S(1)}, u32[]{:S(2)}, u32[]{:S(2)}) collective-permute-start(f32[2,150,128]{2,1,0:T(8,128)S(1)} %dynamic-slice_bitcast_fusion), channel_id=1, source_target_pairs={{0,64},{64,0},{1,65},{65,1},{2,66},{66,2},{3,67},{67,3},{4,68},{68... | collective-permute-start | bytes 460808 | tf_op jit(solution)/shard_map/ppermute | solution.py:17
  137.6 14.8 %collective-permute-start.6 = (f32[50,128]{1,0:T(8,128)S(1)}, f32[50,128]{1,0:T(8,128)S(1)}, u32[]{:S(2)}, u32[]{:S(2)}) collective-permute-start(f32[50,128]{1,0:T(8,128)S(1)} %get-tuple-element.70), channel_id=1, source_target_pairs={{0,128},{128,0},{1,129},{129,1},{2,130},{130,2},{3,131},{131,3},{4... | collective-permute-start | bytes 76808 | tf_op jit(solution)/shard_map/ppermute | solution.py:17
  145.0 9.1 %collective-permute-start.19 = (f32[150,128]{1,0:T(8,128)S(1)}, f32[150,128]{1,0:T(8,128)S(1)}, u32[]{:S(2)}, u32[]{:S(2)}) collective-permute-start(f32[150,128]{1,0:T(8,128)S(1)} %get-tuple-element.64), channel_id=1, source_target_pairs={{0,128},{128,0},{1,129},{129,1},{2,130},{130,2},{3,131},{131,3},{4... | collective-permute-start | bytes 230408 | tf_op jit(solution)/shard_map/ppermute | solution.py:17
  158.9 5.4 %collective-permute-start.20 = (f32[20,640]{1,0:T(8,128)S(1)}, f32[20,640]{1,0:T(8,128)S(1)}, u32[]{:S(2)}, u32[]{:S(2)}) collective-permute-start(f32[20,640]{1,0:T(8,128)S(1)} %squeeze.151), channel_id=1, source_target_pairs={{0,3},{1,0},{2,1},{3,2},{4,7},{5,4},{6,5},{7,6},{8,11},{9,8},{10,9... | collective-permute-start | bytes 153608 | tf_op jit(solution)/shard_map/ppermute | solution.py:17
  163.5 4.7 %collective-permute-start.21 = (f32[20,640]{1,0:T(8,128)S(1)}, f32[20,640]{1,0:T(8,128)S(1)}, u32[]{:S(2)}, u32[]{:S(2)}) collective-permute-start(f32[20,640]{1,0:T(8,128)S(1)} %squeeze.152), channel_id=1, source_target_pairs={{0,2},{1,3},{2,0},{3,1},{4,6},{5,7},{6,4},{7,5},{8,10},{9,11},{10,... | collective-permute-start | bytes 153608 | tf_op jit(solution)/shard_map/ppermute | solution.py:17
  164.1 4.7 %collective-permute-start.22 = (f32[20,640]{1,0:T(8,128)S(1)}, f32[20,640]{1,0:T(8,128)S(1)}, u32[]{:S(2)}, u32[]{:S(2)}) collective-permute-start(f32[20,640]{1,0:T(8,128)S(1)} %squeeze.153), channel_id=1, source_target_pairs={{0,1},{1,2},{2,3},{3,0},{4,5},{5,6},{6,7},{7,4},{8,9},{9,10},{10,1... | collective-permute-start | bytes 153608 | tf_op jit(solution)/shard_map/ppermute | solution.py:17
  170.2 9.4 %copy-start.7 = (f32[1280]{0:T(1024)S(1)}, f32[1280]{0:T(1024)}, u32[]{:S(2)}) copy-start(f32[1280]{0:T(1024)} %param.10) | copy-start | bytes 15364
  171.8 21.5 %collective-permute-start.23 = (f32[5,1280]{1,0:T(8,128)S(1)}, f32[5,1280]{1,0:T(8,128)S(1)}, u32[]{:S(2)}, u32[]{:S(2)}) collective-permute-start(f32[5,1280]{1,0:T(8,128)S(1)} %bitcast.213), channel_id=1, source_target_pairs={{0,192},{64,0},{128,64},{192,128},{1,193},{65,1},{129,65},{193,129... | collective-permute-start | bytes 76808 | tf_op jit(solution)/shard_map/ppermute | solution.py:17
  174.4 18.9 %collective-permute-start.24 = (f32[5,1280]{1,0:T(8,128)S(1)}, f32[5,1280]{1,0:T(8,128)S(1)}, u32[]{:S(2)}, u32[]{:S(2)}) collective-permute-start(f32[5,1280]{1,0:T(8,128)S(1)} %bitcast.214), channel_id=1, source_target_pairs={{0,128},{64,192},{128,0},{192,64},{1,129},{65,193},{129,1},{193,65... | collective-permute-start | bytes 76808 | tf_op jit(solution)/shard_map/ppermute | solution.py:17
  177.4 16.0 %collective-permute-start.25 = (f32[5,1280]{1,0:T(8,128)S(1)}, f32[5,1280]{1,0:T(8,128)S(1)}, u32[]{:S(2)}, u32[]{:S(2)}) collective-permute-start(f32[5,1280]{1,0:T(8,128)S(1)} %bitcast.215), channel_id=1, source_target_pairs={{0,64},{64,128},{128,192},{192,0},{1,65},{65,129},{129,193},{193,1... | collective-permute-start | bytes 76808 | tf_op jit(solution)/shard_map/ppermute | solution.py:17
  180.5 23.9 %all-to-all-start = ((f32[64,1,400]{2,1,0:T(1,128)}), f32[64,1,400]{2,1,0:T(1,128)S(1)}, u32[]{:S(2)}, u32[]{:S(2)}) async-start(f32[64,1,400]{2,1,0:T(1,128)} %copy.563), calls=%async_computation | async-start | bytes 262144 | tf_op jit(solution)/shard_map/all_to_all | solution.py:224
  (5 other events, 6.0 us)

commit v2 on v1

--- a/solution.py
+++ b/solution.py
@@ -187,7 +187,15 @@
 
     total = reduce_x(block([own_left], [own_right])[1])
     pieces = [reduce_z(total)]
-    far_right = tie(far_right, pieces[0][0])
+    turn = (lax.axis_index("y") + jnp.arange(4)) & 3
+    combo = jnp.sum(jnp.where(turn[:, None] == jnp.arange(4)[None], owner[None], 0), axis=1)
+    wanted = jnp.stack([combo, 2 * (combo & 1) + (combo >> 1)], axis=1)[:, :, None, None]
+    mine = combo[:1]
+    first = jnp.where(mine < 2, occ_energy[:1], occ_energy[1:])
+    second = jnp.where((mine & 1) == 0, occ_energy[:1], occ_energy[1:])
+    row_energy = lax.dynamic_slice_in_dim(vir_energy, place_on(ALL) * 20, 20)
+    base = (first + second)[:, None] - row_energy[:, None]
+    far_right, base, wanted = lax.optimization_barrier((far_right, base, wanted, pieces[0][0]))[:3]
     keep, parts_a = block([own_left], [far_right])
     total_a = reduce_x(parts_a)
     far_left = tie(far_left, keep)
@@ -197,9 +205,6 @@
     full = assemble(places, pieces)
     full = full.reshape(2, 10, 2, 2, 320)
 
-    turn = (lax.axis_index("y") + jnp.arange(4)) & 3
-    combo = jnp.sum(jnp.where(turn[:, None] == jnp.arange(4)[None], owner[None], 0), axis=1)
-    wanted = jnp.stack([combo, 2 * (combo & 1) + (combo >> 1)], axis=1)[:, :, None, None]
     by_pair = [full[i, :, :, j].reshape(10, 640) for i in range(2) for j in range(2)]
     got = jnp.where(
         wanted < 2,
@@ -227,11 +232,7 @@
     direct = exchange_ring([take(home, (me + r) & 3) for r in range(4)], ("zh", "zm"))
     direct = direct.transpose(1, 0, 2).reshape(20, 1280)
 
-    mine = combo[:1]
-    first = jnp.where(mine < 2, occ_energy[:1], occ_energy[1:])
-    second = jnp.where((mine & 1) == 0, occ_energy[:1], occ_energy[1:])
-    row_energy = lax.dynamic_slice_in_dim(vir_energy, place_on(ALL) * 20, 20)
-    gap = (first + second)[:, None] - row_energy[:, None] - vir_energy[None, :]
+    gap = base - vir_energy[None, :]
     return ((direct + mirrored) / gap)[None]
 
 

time: 207 us -> 204 us (0.986)
    unnamed x31 -> x29, local copies, waits for them, and re-layouts: 6.4 us -> 5.75 us
  transfers between devices with their start and end apart: 27 -> 27, of which waited for: 20 -> 20; matrix products, arithmetic and copies ran while one was open for 5% -> 4% of each run, Pallas kernels for 6% -> 6%
where the time goes in v2:
time: 204 us
  waiting for transfers between devices  90.5 us (44%)
  starting transfers between devices  66.8 us (33%)
  Pallas kernels  22 us (11%)
  local copies, waits for them, and re-layouts  16.4 us (8%)
  other arithmetic  4.77 us (2%)
  between operations  3.39 us (2%)
    ppermute x26, waiting for transfers between devices, permute(): lax.ppermute(value, axis, [(s, target(s)) for s in range(lax.axis_size(ax...  79.9 us
    ppermute x26, starting transfers between devices, permute(): lax.ppermute(value, axis, [(s, target(s)) for s in range(lax.axis_size(ax...  53.9 us
    pallas_call x3, Pallas kernels, product(): pl.pallas_call(functools.partial(product_kernel, jobs, len(left), len(rig...  18 us
    all_to_all x1, starting transfers between devices, body(): lax.all_to_all(swapped, ALL, split_axis=0, concat_axis=0, tiled=True)  12.8 us
    all_to_all x1, waiting for transfers between devices, body(): lax.all_to_all(swapped, ALL, split_axis=0, concat_axis=0, tiled=True)  10.6 us
    unnamed x29, local copies, waits for them, and re-layouts  5.75 us
  transfers between devices with their start and end apart: 27, of which 20 were waited for; matrix products, arithmetic and copies ran while one was open for 4% of the time, Pallas kernels for 6%

profile of v2, /device:TPU:1, one launch (start us, length us, event | category | flops | bytes accessed | tf_op | source)
XLA Modules:
  0.0 203.7 jit_solution(10536566696961767193)
XLA Ops:
  0.0 3.6 %collective-permute-start = (bf16[4,640,640]{2,1,0:T(8,128)(2,1)}, bf16[4,640,640]{2,1,0:T(8,128)(2,1)}, u32[]{:S(2)}, u32[]{:S(2)}) collective-permute-start(bf16[4,640,640]{2,1,0:T(8,128)(2,1)} %bitcast.206), channel_id=1, source_target_pairs={{0,3},{1,2},{2,1},{3,0},{4,7},{5,6},{6,5},{7,4},{8,11},{9,10},{10,... | collective-permute-start | bytes 9830408 | tf_op jit(solution)/shard_map/ppermute | solution.py:17
  4.6 1.9 copy-done.2
  6.5 2.2 %shard_map.64.refs_0_ = bf16[5,4,128,640]{3,2,1,0:T(8,128)(2,1)S(1)} custom-call(bf16[2,5,4,640]{3,2,1,0:T(4,128)(2,1)S(1)} %convert_element_type.34.mask_ref, bf16[2,2,8,5,4,4,640]{6,5,4,3,2,1,0:T(4,128)(2,1)S(1)} %bitcast.209), custom_call_target="tpu_custom_call" | custom-call | flops 1 | bytes 1 | tf_op jit(solution)/shard_map/pallas_call | solution.py:41
  10.8 4.0 %shard_map.65 = (f32[4,25,16,128]{3,2,1,0:T(8,128)S(1)}, f32[4,25,16,128]{3,2,1,0:T(8,128)}) custom-call(s32[1]{0:T(128)} %bitcast.6.core_ref, bf16[5,4,128,640]{3,2,1,0:T(8,128)(2,1)S(1)} %shard_map.64.refs_0_, bf16[4,640,640]{2,1,0:T(8,128)(2,1)S(1)} %bitcast.207), custom_call_target="tpu_custom_call" | custom-call | flops 1 | bytes 1 | tf_op jit(solution)/shard_map/pallas_call | solution.py:95
  23.3 2.5 %collective-permute-start.3 = (f32[25,16,128]{2,1,0:T(8,128)S(1)}, f32[25,16,128]{2,1,0:T(8,128)S(1)}, u32[]{:S(2)}, u32[]{:S(2)}) collective-permute-start(f32[25,16,128]{2,1,0:T(8,128)S(1)} %get-tuple-element.44), channel_id=1, source_target_pairs={{0,16},{8,24},{16,0},{24,8},{1,17},{9,25},{17,1},{25,9},{2,18},{10... | collective-permute-start | bytes 614408 | tf_op jit(solution)/shard_map/ppermute | solution.py:17
  26.9 3.2 %collective-permute-done.2 = f32[25,16,128]{2,1,0:T(8,128)S(1)} collective-permute-done((f32[25,16,128]{2,1,0:T(8,128)S(1)}, f32[25,16,128]{2,1,0:T(8,128)S(1)}, u32[]{:S(2)}, u32[]{:S(2)}) %collective-permute-start.2) | collective-permute-done | bytes 204832 | tf_op jit(solution)/shard_map/ppermute | solution.py:17
  30.1 5.3 %collective-permute-done.3 = f32[25,16,128]{2,1,0:T(8,128)S(1)} collective-permute-done((f32[25,16,128]{2,1,0:T(8,128)S(1)}, f32[25,16,128]{2,1,0:T(8,128)S(1)}, u32[]{:S(2)}, u32[]{:S(2)}) %collective-permute-start.3) | collective-permute-done | bytes 204832 | tf_op jit(solution)/shard_map/ppermute | solution.py:17
  38.3 2.7 %collective-permute-done.5 = f32[2,2,50,128]{3,2,1,0:T(8,128)S(1)} collective-permute-done((f32[2,2,50,128]{3,2,1,0:T(8,128)S(1)}, f32[2,2,50,128]{3,2,1,0:T(8,128)S(1)}, u32[]{:S(2)}, u32[]{:S(2)}) %collective-permute-start.5) | collective-permute-done | bytes 102432 | tf_op jit(solution)/shard_map/ppermute | solution.py:17
  41.0 3.3 %collective-permute-start.6 = (f32[2,50,128]{2,1,0:T(8,128)S(1)}, f32[2,50,128]{2,1,0:T(8,128)S(1)}, u32[]{:S(2)}, u32[]{:S(2)}) collective-permute-start(f32[2,50,128]{2,1,0:T(8,128)S(1)} %dynamic-slice_bitcast_fusion.4), channel_id=1, source_target_pairs={{0,64},{64,0},{1,65},{65,1},{2,66},{66,2},{3,67},{67,3},{4,68},{68... | collective-permute-start | bytes 153608 | tf_op jit(solution)/shard_map/ppermute | solution.py:17
  46.9 26.6 %collective-permute-done.refs_1_.refs_2_ = bf16[4,640,640]{2,1,0:T(8,128)(2,1)} collective-permute-done((bf16[4,640,640]{2,1,0:T(8,128)(2,1)}, bf16[4,640,640]{2,1,0:T(8,128)(2,1)}, u32[]{:S(2)}, u32[]{:S(2)}) %collective-permute-start) | collective-permute-done | bytes 3276832 | tf_op jit(solution)/shard_map/ppermute | solution.py:17
  73.5 5.1 %shard_map.66 = (f32[4,25,16,128]{3,2,1,0:T(8,128)S(1)}, f32[4,25,16,128]{3,2,1,0:T(8,128)S(1)}) custom-call(s32[1]{0:T(128)} %bitcast.6.core_ref, bf16[5,4,128,640]{3,2,1,0:T(8,128)(2,1)S(1)} %shard_map.64.refs_0_, bf16[4,640,640]{2,1,0:T(8,128)(2,1)} %collective-permute-done.refs_1_.refs_2_), custom_call_target="tpu_custom_call" | custom-call | flops 1 | bytes 1 | tf_op jit(solution)/shard_map/pallas_call | solution.py:95
  80.4 8.9 %shard_map.67 = (f32[4,50,16,128]{3,2,1,0:T(8,128)S(1)}, f32[4,50,16,128]{3,2,1,0:T(8,128)S(1)}) custom-call(s32[1]{0:T(128)} %bitcast.6.core_ref, bf16[5,4,128,640]{3,2,1,0:T(8,128)(2,1)} %collective-permute-done.12.refs_0_, bf16[4,640,640]{2,1,0:T(8,128)(2,1)S(1)} %bitcast.208, bf16[4,640,640]{2,1,0:T(8,128)(2,1)} %collective-permute-done.refs_1_.refs_2_), custom_call_target="tpu_custom_call" | custom-call | flops 1 | bytes 1 | tf_op jit(solution)/shard_map/pallas_call | solution.py:95
  89.3 1.9 collective-permute-start.13
  91.4 4.2 %collective-permute-done.8 = f32[4,25,16,128]{3,2,1,0:T(8,128)S(1)} collective-permute-done((f32[4,25,16,128]{3,2,1,0:T(8,128)S(1)}, f32[4,25,16,128]{3,2,1,0:T(8,128)S(1)}, u32[]{:S(2)}, u32[]{:S(2)}) %collective-permute-start.8) | collective-permute-done | bytes 819232 | tf_op jit(solution)/shard_map/ppermute | solution.py:17
  95.6 2.8 %collective-permute-start.10 = (f32[25,16,128]{2,1,0:T(8,128)S(1)}, f32[25,16,128]{2,1,0:T(8,128)S(1)}, u32[]{:S(2)}, u32[]{:S(2)}) collective-permute-start(f32[25,16,128]{2,1,0:T(8,128)S(1)} %get-tuple-element.41), channel_id=1, source_target_pairs={{0,16},{8,24},{16,0},{24,8},{1,17},{9,25},{17,1},{25,9},{2,18},{10... | collective-permute-start | bytes 614408 | tf_op jit(solution)/shard_map/ppermute | solution.py:17
  100.5 2.9 %collective-permute-start.15 = (f32[50,16,128]{2,1,0:T(8,128)S(1)}, f32[50,16,128]{2,1,0:T(8,128)S(1)}, u32[]{:S(2)}, u32[]{:S(2)}) collective-permute-start(f32[50,16,128]{2,1,0:T(8,128)S(1)} %get-tuple-element.38), channel_id=1, source_target_pairs={{0,16},{8,24},{16,0},{24,8},{1,17},{9,25},{17,1},{25,9},{2,18},{10... | collective-permute-start | bytes 1228808 | tf_op jit(solution)/shard_map/ppermute | solution.py:17
  103.5 2.5 %collective-permute-start.16 = (f32[50,16,128]{2,1,0:T(8,128)S(1)}, f32[50,16,128]{2,1,0:T(8,128)S(1)}, u32[]{:S(2)}, u32[]{:S(2)}) collective-permute-start(f32[50,16,128]{2,1,0:T(8,128)S(1)} %get-tuple-element.37), channel_id=1, source_target_pairs={{0,24},{8,0},{16,8},{24,16},{1,25},{9,1},{17,9},{25,17},{2,26},{10... | collective-permute-start | bytes 1228808 | tf_op jit(solution)/shard_map/ppermute | solution.py:17
  106.0 2.0 collective-permute-done.11
  108.2 8.9 %collective-permute-done.14 = f32[50,16,128]{2,1,0:T(8,128)S(1)} collective-permute-done((f32[50,16,128]{2,1,0:T(8,128)S(1)}, f32[50,16,128]{2,1,0:T(8,128)S(1)}, u32[]{:S(2)}, u32[]{:S(2)}) %collective-permute-start.14) | collective-permute-done | bytes 409632 | tf_op jit(solution)/shard_map/ppermute | solution.py:17
  117.1 8.4 %collective-permute-done.15 = f32[50,16,128]{2,1,0:T(8,128)S(1)} collective-permute-done((f32[50,16,128]{2,1,0:T(8,128)S(1)}, f32[50,16,128]{2,1,0:T(8,128)S(1)}, u32[]{:S(2)}, u32[]{:S(2)}) %collective-permute-start.15) | collective-permute-done | bytes 409632 | tf_op jit(solution)/shard_map/ppermute | solution.py:17
  126.1 1.9 collective-permute-start.17
  128.0 6.4 %collective-permute-done.17 = f32[2,2,150,128]{3,2,1,0:T(8,128)S(1)} collective-permute-done((f32[2,2,150,128]{3,2,1,0:T(8,128)S(1)}, f32[2,2,150,128]{3,2,1,0:T(8,128)S(1)}, u32[]{:S(2)}, u32[]{:S(2)}) %collective-permute-start.17) | collective-permute-done | bytes 307232 | tf_op jit(solution)/shard_map/ppermute | solution.py:17
  134.5 3.1 %collective-permute-start.18 = (f32[2,150,128]{2,1,0:T(8,128)S(1)}, f32[2,150,128]{2,1,0:T(8,128)S(1)}, u32[]{:S(2)}, u32[]{:S(2)}) collective-permute-start(f32[2,150,128]{2,1,0:T(8,128)S(1)} %dynamic-slice_bitcast_fusion), channel_id=1, source_target_pairs={{0,64},{64,0},{1,65},{65,1},{2,66},{66,2},{3,67},{67,3},{4,68},{68... | collective-permute-start | bytes 460808 | tf_op jit(solution)/shard_map/ppermute | solution.py:17
  137.5 4.8 %collective-permute-start.7 = (f32[50,128]{1,0:T(8,128)S(1)}, f32[50,128]{1,0:T(8,128)S(1)}, u32[]{:S(2)}, u32[]{:S(2)}) collective-permute-start(f32[50,128]{1,0:T(8,128)S(1)} %get-tuple-element.74), channel_id=1, source_target_pairs={{0,128},{128,0},{1,129},{129,1},{2,130},{130,2},{3,131},{131,3},{4... | collective-permute-start | bytes 76808 | tf_op jit(solution)/shard_map/ppermute | solution.py:17
  142.3 2.0 collective-permute-done.18
  145.0 7.3 %collective-permute-start.19 = (f32[150,128]{1,0:T(8,128)S(1)}, f32[150,128]{1,0:T(8,128)S(1)}, u32[]{:S(2)}, u32[]{:S(2)}) collective-permute-start(f32[150,128]{1,0:T(8,128)S(1)} %get-tuple-element.68), channel_id=1, source_target_pairs={{0,128},{128,0},{1,129},{129,1},{2,130},{130,2},{3,131},{131,3},{4... | collective-permute-start | bytes 230408 | tf_op jit(solution)/shard_map/ppermute | solution.py:17
  162.0 3.0 %collective-permute-done.21 = f32[20,640]{1,0:T(8,128)S(1)} collective-permute-done((f32[20,640]{1,0:T(8,128)S(1)}, f32[20,640]{1,0:T(8,128)S(1)}, u32[]{:S(2)}, u32[]{:S(2)}) %collective-permute-start.21) | collective-permute-done | bytes 51232 | tf_op jit(solution)/shard_map/ppermute | solution.py:17
  168.5 2.6 %collective-permute-start.23 = (f32[5,1280]{1,0:T(8,128)S(1)}, f32[5,1280]{1,0:T(8,128)S(1)}, u32[]{:S(2)}, u32[]{:S(2)}) collective-permute-start(f32[5,1280]{1,0:T(8,128)S(1)} %bitcast.225), channel_id=1, source_target_pairs={{0,192},{64,0},{128,64},{192,128},{1,193},{65,1},{129,65},{193,129... | collective-permute-start | bytes 76808 | tf_op jit(solution)/shard_map/ppermute | solution.py:17
  171.2 2.9 %collective-permute-start.24 = (f32[5,1280]{1,0:T(8,128)S(1)}, f32[5,1280]{1,0:T(8,128)S(1)}, u32[]{:S(2)}, u32[]{:S(2)}) collective-permute-start(f32[5,1280]{1,0:T(8,128)S(1)} %bitcast.226), channel_id=1, source_target_pairs={{0,128},{64,192},{128,0},{192,64},{1,129},{65,193},{129,1},{193,65... | collective-permute-start | bytes 76808 | tf_op jit(solution)/shard_map/ppermute | solution.py:17
  174.1 2.3 %collective-permute-start.25 = (f32[5,1280]{1,0:T(8,128)S(1)}, f32[5,1280]{1,0:T(8,128)S(1)}, u32[]{:S(2)}, u32[]{:S(2)}) collective-permute-start(f32[5,1280]{1,0:T(8,128)S(1)} %bitcast.227), channel_id=1, source_target_pairs={{0,64},{64,128},{128,192},{192,0},{1,65},{65,129},{129,193},{193,1... | collective-permute-start | bytes 76808 | tf_op jit(solution)/shard_map/ppermute | solution.py:17
  177.1 12.8 %all-to-all-start = ((f32[64,1,400]{2,1,0:T(1,128)}), f32[64,1,400]{2,1,0:T(1,128)S(1)}, u32[]{:S(2)}, u32[]{:S(2)}) async-start(f32[64,1,400]{2,1,0:T(1,128)} %copy.659), calls=%async_computation | async-start | bytes 262144 | tf_op jit(solution)/shard_map/all_to_all | solution.py:229
  190.5 10.6 %all-to-all-done = f32[64,1,400]{2,1,0:T(1,128)S(1)} async-done(((f32[64,1,400]{2,1,0:T(1,128)}), f32[64,1,400]{2,1,0:T(1,128)S(1)}, u32[]{:S(2)}, u32[]{:S(2)}) %all-to-all-start) | async-done | bytes 102432 | tf_op jit(solution)/shard_map/all_to_all | solution.py:229
  (131 shorter events, 37.8 us)
Async XLA Ops:
  0.0 73.5 %collective-permute-start = (bf16[4,640,640]{2,1,0:T(8,128)(2,1)}, bf16[4,640,640]{2,1,0:T(8,128)(2,1)}, u32[]{:S(2)}, u32[]{:S(2)}) collective-permute-start(bf16[4,640,640]{2,1,0:T(8,128)(2,1)} %bitcast.206), channel_id=1, source_target_pairs={{0,3},{1,2},{2,1},{3,0},{4,7},{5,6},{6,5},{7,4},{8,11},{9,10},{10,... | collective-permute-start | bytes 9830408 | tf_op jit(solution)/shard_map/ppermute | solution.py:17
  4.6 1.9 copy-start.2
  8.8 71.7 %collective-permute-start.12 = (bf16[5,4,128,640]{3,2,1,0:T(8,128)(2,1)S(1)}, bf16[5,4,128,640]{3,2,1,0:T(8,128)(2,1)}, u32[]{:S(2)}, u32[]{:S(2)}) collective-permute-start(bf16[5,4,128,640]{3,2,1,0:T(8,128)(2,1)S(1)} %shard_map.64.refs_0_), channel_id=1, source_target_pairs={{0,1},{1,0},{2,3},{3,2},{4,5},{5,4},{6,7},{7,6},{8,9},{9,8},{10,11... | collective-permute-start | bytes 9830408 | tf_op jit(solution)/shard_map/ppermute | solution.py:17
  10.8 6.0 %copy-start.8 = (s32[4]{0:T(128)S(1)}, s32[4]{0:T(128)}, u32[]{:S(2)}) copy-start(s32[4]{0:T(128)} %param.11) | copy-start | bytes 52
  10.8 6.3 %copy-start.7 = (f32[2]{0:T(128)S(1)}, f32[2]{0:T(128)}, u32[]{:S(2)}) copy-start(f32[2]{0:T(128)} %param.9) | copy-start | bytes 28
  15.7 4.8 %collective-permute-start.1 = (f32[4,25,16,128]{3,2,1,0:T(8,128)}, f32[4,25,16,128]{3,2,1,0:T(8,128)}, u32[]{:S(2)}, u32[]{:S(2)}) collective-permute-start(f32[4,25,16,128]{3,2,1,0:T(8,128)} %get-tuple-element.18), channel_id=1, source_target_pairs={{0,4},{4,0},{1,5},{5,1},{2,6},{6,2},{3,7},{7,3},{8,12},{12,8},{9,1... | collective-permute-start | bytes 2457608 | tf_op jit(solution)/shard_map/ppermute | solution.py:17
  20.5 23.8 %copy-start.6 = (f32[1280]{0:T(1024)S(1)}, f32[1280]{0:T(1024)}, u32[]{:S(2)}) copy-start(f32[1280]{0:T(1024)} %param.10) | copy-start | bytes 15364
  22.0 8.1 %collective-permute-start.2 = (f32[25,16,128]{2,1,0:T(8,128)S(1)}, f32[25,16,128]{2,1,0:T(8,128)S(1)}, u32[]{:S(2)}, u32[]{:S(2)}) collective-permute-start(f32[25,16,128]{2,1,0:T(8,128)S(1)} %get-tuple-element.42), channel_id=1, source_target_pairs={{0,8},{8,16},{16,24},{24,0},{1,9},{9,17},{17,25},{25,1},{2,10},{10... | collective-permute-start | bytes 614408 | tf_op jit(solution)/shard_map/ppermute | solution.py:17
  23.3 12.1 %collective-permute-start.3 = (f32[25,16,128]{2,1,0:T(8,128)S(1)}, f32[25,16,128]{2,1,0:T(8,128)S(1)}, u32[]{:S(2)}, u32[]{:S(2)}) collective-permute-start(f32[25,16,128]{2,1,0:T(8,128)S(1)} %get-tuple-element.44), channel_id=1, source_target_pairs={{0,16},{8,24},{16,0},{24,8},{1,17},{9,25},{17,1},{25,9},{2,18},{10... | collective-permute-start | bytes 614408 | tf_op jit(solution)/shard_map/ppermute | solution.py:17
  25.7 9.6 %collective-permute-start.4 = (f32[25,16,128]{2,1,0:T(8,128)S(1)}, f32[25,16,128]{2,1,0:T(8,128)S(1)}, u32[]{:S(2)}, u32[]{:S(2)}) collective-permute-start(f32[25,16,128]{2,1,0:T(8,128)S(1)} %get-tuple-element.43), channel_id=1, source_target_pairs={{0,24},{8,0},{16,8},{24,16},{1,25},{9,1},{17,9},{25,17},{2,26},{10... | collective-permute-start | bytes 614408 | tf_op jit(solution)/shard_map/ppermute | solution.py:17
  36.5 4.5 %collective-permute-start.5 = (f32[2,2,50,128]{3,2,1,0:T(8,128)S(1)}, f32[2,2,50,128]{3,2,1,0:T(8,128)S(1)}, u32[]{:S(2)}, u32[]{:S(2)}) collective-permute-start(f32[2,2,50,128]{3,2,1,0:T(8,128)S(1)} %bitcast.224), channel_id=1, source_target_pairs={{0,32},{32,0},{1,33},{33,1},{2,34},{34,2},{3,35},{35,3},{4,36},{36... | collective-permute-start | bytes 307208 | tf_op jit(solution)/shard_map/ppermute | solution.py:17
  41.0 5.2 %collective-permute-start.6 = (f32[2,50,128]{2,1,0:T(8,128)S(1)}, f32[2,50,128]{2,1,0:T(8,128)S(1)}, u32[]{:S(2)}, u32[]{:S(2)}) collective-permute-start(f32[2,50,128]{2,1,0:T(8,128)S(1)} %dynamic-slice_bitcast_fusion.4), channel_id=1, source_target_pairs={{0,64},{64,0},{1,65},{65,1},{2,66},{66,2},{3,67},{67,3},{4,68},{68... | collective-permute-start | bytes 153608 | tf_op jit(solution)/shard_map/ppermute | solution.py:17
  73.5 7.0 %copy-start.1 = (bf16[4,640,2,320]{1,3,2,0:T(8,128)(2,1)S(1)}, bf16[4,640,2,320]{1,3,2,0:T(8,128)(2,1)}, u32[]{:S(2)}) copy-start(bf16[4,640,2,320]{1,3,2,0:T(8,128)(2,1)} %param.7) | copy-start | bytes 9830404
  89.3 10.6 %collective-permute-start.13 = (f32[4,50,16,128]{3,2,1,0:T(8,128)S(1)}, f32[4,50,16,128]{3,2,1,0:T(8,128)S(1)}, u32[]{:S(2)}, u32[]{:S(2)}) collective-permute-start(f32[4,50,16,128]{3,2,1,0:T(8,128)S(1)} %get-tuple-element.25), channel_id=1, source_target_pairs={{0,4},{4,0},{1,5},{5,1},{2,6},{6,2},{3,7},{7,3},{8,12},{12,8},{9,1... | collective-permute-start | bytes 4915208 | tf_op jit(solution)/shard_map/ppermute | solution.py:17
  91.3 4.3 %collective-permute-start.8 = (f32[4,25,16,128]{3,2,1,0:T(8,128)S(1)}, f32[4,25,16,128]{3,2,1,0:T(8,128)S(1)}, u32[]{:S(2)}, u32[]{:S(2)}) collective-permute-start(f32[4,25,16,128]{3,2,1,0:T(8,128)S(1)} %get-tuple-element.22), channel_id=1, source_target_pairs={{0,4},{4,0},{1,5},{5,1},{2,6},{6,2},{3,7},{7,3},{8,12},{12,8},{9,1... | collective-permute-start | bytes 2457608 | tf_op jit(solution)/shard_map/ppermute | solution.py:17
  95.6 7.9 %collective-permute-start.10 = (f32[25,16,128]{2,1,0:T(8,128)S(1)}, f32[25,16,128]{2,1,0:T(8,128)S(1)}, u32[]{:S(2)}, u32[]{:S(2)}) collective-permute-start(f32[25,16,128]{2,1,0:T(8,128)S(1)} %get-tuple-element.41), channel_id=1, source_target_pairs={{0,16},{8,24},{16,0},{24,8},{1,17},{9,25},{17,1},{25,9},{2,18},{10... | collective-permute-start | bytes 614408 | tf_op jit(solution)/shard_map/ppermute | solution.py:17
  98.5 9.6 %collective-permute-start.11 = (f32[25,16,128]{2,1,0:T(8,128)S(1)}, f32[25,16,128]{2,1,0:T(8,128)S(1)}, u32[]{:S(2)}, u32[]{:S(2)}) collective-permute-start(f32[25,16,128]{2,1,0:T(8,128)S(1)} %get-tuple-element.40), channel_id=1, source_target_pairs={{0,24},{8,0},{16,8},{24,16},{1,25},{9,1},{17,9},{25,17},{2,26},{10... | collective-permute-start | bytes 614408 | tf_op jit(solution)/shard_map/ppermute | solution.py:17
  99.3 8.8 %collective-permute-start.9 = (f32[25,16,128]{2,1,0:T(8,128)S(1)}, f32[25,16,128]{2,1,0:T(8,128)S(1)}, u32[]{:S(2)}, u32[]{:S(2)}) collective-permute-start(f32[25,16,128]{2,1,0:T(8,128)S(1)} %get-tuple-element.39), channel_id=1, source_target_pairs={{0,8},{8,16},{16,24},{24,0},{1,9},{9,17},{17,25},{25,1},{2,10},{10... | collective-permute-start | bytes 614408 | tf_op jit(solution)/shard_map/ppermute | solution.py:17
  100.1 17.0 %collective-permute-start.14 = (f32[50,16,128]{2,1,0:T(8,128)S(1)}, f32[50,16,128]{2,1,0:T(8,128)S(1)}, u32[]{:S(2)}, u32[]{:S(2)}) collective-permute-start(f32[50,16,128]{2,1,0:T(8,128)S(1)} %get-tuple-element.36), channel_id=1, source_target_pairs={{0,8},{8,16},{16,24},{24,0},{1,9},{9,17},{17,25},{25,1},{2,10},{10... | collective-permute-start | bytes 1228808 | tf_op jit(solution)/shard_map/ppermute | solution.py:17
  100.5 25.0 %collective-permute-start.15 = (f32[50,16,128]{2,1,0:T(8,128)S(1)}, f32[50,16,128]{2,1,0:T(8,128)S(1)}, u32[]{:S(2)}, u32[]{:S(2)}) collective-permute-start(f32[50,16,128]{2,1,0:T(8,128)S(1)} %get-tuple-element.38), channel_id=1, source_target_pairs={{0,16},{8,24},{16,0},{24,8},{1,17},{9,25},{17,1},{25,9},{2,18},{10... | collective-permute-start | bytes 1228808 | tf_op jit(solution)/shard_map/ppermute | solution.py:17
  103.5 22.1 %collective-permute-start.16 = (f32[50,16,128]{2,1,0:T(8,128)S(1)}, f32[50,16,128]{2,1,0:T(8,128)S(1)}, u32[]{:S(2)}, u32[]{:S(2)}) collective-permute-start(f32[50,16,128]{2,1,0:T(8,128)S(1)} %get-tuple-element.37), channel_id=1, source_target_pairs={{0,24},{8,0},{16,8},{24,16},{1,25},{9,1},{17,9},{25,17},{2,26},{10... | collective-permute-start | bytes 1228808 | tf_op jit(solution)/shard_map/ppermute | solution.py:17
  126.1 8.3 %collective-permute-start.17 = (f32[2,2,150,128]{3,2,1,0:T(8,128)S(1)}, f32[2,2,150,128]{3,2,1,0:T(8,128)S(1)}, u32[]{:S(2)}, u32[]{:S(2)}) collective-permute-start(f32[2,2,150,128]{3,2,1,0:T(8,128)S(1)} %bitcast.219), channel_id=1, source_target_pairs={{0,32},{32,0},{1,33},{33,1},{2,34},{34,2},{3,35},{35,3},{4,36},{36... | collective-permute-start | bytes 921608 | tf_op jit(solution)/shard_map/ppermute | solution.py:17
  134.5 9.8 %collective-permute-start.18 = (f32[2,150,128]{2,1,0:T(8,128)S(1)}, f32[2,150,128]{2,1,0:T(8,128)S(1)}, u32[]{:S(2)}, u32[]{:S(2)}) collective-permute-start(f32[2,150,128]{2,1,0:T(8,128)S(1)} %dynamic-slice_bitcast_fusion), channel_id=1, source_target_pairs={{0,64},{64,0},{1,65},{65,1},{2,66},{66,2},{3,67},{67,3},{4,68},{68... | collective-permute-start | bytes 460808 | tf_op jit(solution)/shard_map/ppermute | solution.py:17
  137.5 14.8 %collective-permute-start.7 = (f32[50,128]{1,0:T(8,128)S(1)}, f32[50,128]{1,0:T(8,128)S(1)}, u32[]{:S(2)}, u32[]{:S(2)}) collective-permute-start(f32[50,128]{1,0:T(8,128)S(1)} %get-tuple-element.74), channel_id=1, source_target_pairs={{0,128},{128,0},{1,129},{129,1},{2,130},{130,2},{3,131},{131,3},{4... | collective-permute-start | bytes 76808 | tf_op jit(solution)/shard_map/ppermute | solution.py:17
  145.0 9.1 %collective-permute-start.19 = (f32[150,128]{1,0:T(8,128)S(1)}, f32[150,128]{1,0:T(8,128)S(1)}, u32[]{:S(2)}, u32[]{:S(2)}) collective-permute-start(f32[150,128]{1,0:T(8,128)S(1)} %get-tuple-element.68), channel_id=1, source_target_pairs={{0,128},{128,0},{1,129},{129,1},{2,130},{130,2},{3,131},{131,3},{4... | collective-permute-start | bytes 230408 | tf_op jit(solution)/shard_map/ppermute | solution.py:17
  158.8 3.1 %collective-permute-start.20 = (f32[20,640]{1,0:T(8,128)S(1)}, f32[20,640]{1,0:T(8,128)S(1)}, u32[]{:S(2)}, u32[]{:S(2)}) collective-permute-start(f32[20,640]{1,0:T(8,128)S(1)} %squeeze.151), channel_id=1, source_target_pairs={{0,3},{1,0},{2,1},{3,2},{4,7},{5,4},{6,5},{7,6},{8,11},{9,8},{10,9... | collective-permute-start | bytes 153608 | tf_op jit(solution)/shard_map/ppermute | solution.py:17
  160.2 4.7 %collective-permute-start.21 = (f32[20,640]{1,0:T(8,128)S(1)}, f32[20,640]{1,0:T(8,128)S(1)}, u32[]{:S(2)}, u32[]{:S(2)}) collective-permute-start(f32[20,640]{1,0:T(8,128)S(1)} %squeeze.152), channel_id=1, source_target_pairs={{0,2},{1,3},{2,0},{3,1},{4,6},{5,7},{6,4},{7,5},{8,10},{9,11},{10,... | collective-permute-start | bytes 153608 | tf_op jit(solution)/shard_map/ppermute | solution.py:17
  160.8 4.7 %collective-permute-start.22 = (f32[20,640]{1,0:T(8,128)S(1)}, f32[20,640]{1,0:T(8,128)S(1)}, u32[]{:S(2)}, u32[]{:S(2)}) collective-permute-start(f32[20,640]{1,0:T(8,128)S(1)} %squeeze.153), channel_id=1, source_target_pairs={{0,1},{1,2},{2,3},{3,0},{4,5},{5,6},{6,7},{7,4},{8,9},{9,10},{10,1... | collective-permute-start | bytes 153608 | tf_op jit(solution)/shard_map/ppermute | solution.py:17
  168.5 21.4 %collective-permute-start.23 = (f32[5,1280]{1,0:T(8,128)S(1)}, f32[5,1280]{1,0:T(8,128)S(1)}, u32[]{:S(2)}, u32[]{:S(2)}) collective-permute-start(f32[5,1280]{1,0:T(8,128)S(1)} %bitcast.225), channel_id=1, source_target_pairs={{0,192},{64,0},{128,64},{192,128},{1,193},{65,1},{129,65},{193,129... | collective-permute-start | bytes 76808 | tf_op jit(solution)/shard_map/ppermute | solution.py:17
  171.2 18.8 %collective-permute-start.24 = (f32[5,1280]{1,0:T(8,128)S(1)}, f32[5,1280]{1,0:T(8,128)S(1)}, u32[]{:S(2)}, u32[]{:S(2)}) collective-permute-start(f32[5,1280]{1,0:T(8,128)S(1)} %bitcast.226), channel_id=1, source_target_pairs={{0,128},{64,192},{128,0},{192,64},{1,129},{65,193},{129,1},{193,65... | collective-permute-start | bytes 76808 | tf_op jit(solution)/shard_map/ppermute | solution.py:17
  174.1 15.9 %collective-permute-start.25 = (f32[5,1280]{1,0:T(8,128)S(1)}, f32[5,1280]{1,0:T(8,128)S(1)}, u32[]{:S(2)}, u32[]{:S(2)}) collective-permute-start(f32[5,1280]{1,0:T(8,128)S(1)} %bitcast.227), channel_id=1, source_target_pairs={{0,64},{64,128},{128,192},{192,0},{1,65},{65,129},{129,193},{193,1... | collective-permute-start | bytes 76808 | tf_op jit(solution)/shard_map/ppermute | solution.py:17
  177.1 23.9 %all-to-all-start = ((f32[64,1,400]{2,1,0:T(1,128)}), f32[64,1,400]{2,1,0:T(1,128)S(1)}, u32[]{:S(2)}, u32[]{:S(2)}) async-start(f32[64,1,400]{2,1,0:T(1,128)} %copy.659), calls=%async_computation | async-start | bytes 262144 | tf_op jit(solution)/shard_map/all_to_all | solution.py:229
  (4 other events, 5.3 us)

commit v3 on v2

--- a/solution.py
+++ b/solution.py
@@ -106,7 +106,7 @@
     got = permute(send, "core", lambda s: 1 - s)
     mine = place_on("x")
     spots = [mine, (mine + 1) & 3, (mine + 2) & 3, (mine + 3) & 3]
-    return [take(keep, at) + take(got, at) for at in spots]
+    return got, [take(keep, at) + take(got, at) for at in spots]
 
 
 def reduce_x(parts):
@@ -183,7 +183,7 @@
     def block(left, right):
         pairs = [(l, r) for l in range(len(left)) for r in range(len(right))]
         keep, send = product(core, left, right, pairs)
-        return keep, reduce_chip(keep, send)
+        return reduce_chip(keep, send)
 
     total = reduce_x(block([own_left], [own_right])[1])
     pieces = [reduce_z(total)]
@@ -196,9 +196,9 @@
     row_energy = lax.dynamic_slice_in_dim(vir_energy, place_on(ALL) * 20, 20)
     base = (first + second)[:, None] - row_energy[:, None]
     far_right, base, wanted = lax.optimization_barrier((far_right, base, wanted, pieces[0][0]))[:3]
-    keep, parts_a = block([own_left], [far_right])
+    got_a, parts_a = block([own_left], [far_right])
     total_a = reduce_x(parts_a)
-    far_left = tie(far_left, keep)
+    far_left = tie(far_left, got_a)
     total_b = reduce_x(block([far_left], [own_right, far_right])[1])
     pieces.append(reduce_z(jnp.concatenate([total_a, total_b])))
     places = [cells_of(0, 0), cells_of(0, 1) + cells_of(1, 0) + cells_of(1, 1)]

time: 204 us -> 202 us (level)
  waiting for transfers between devices: 90.5 us -> 87.1 us
    ppermute x26, waiting for transfers between devices: 79.9 us -> 76.5 us  [permute(): lax.ppermute(value, axis, [(s, target(s)) for s in range(lax.axis_size(ax...]
  transfers between devices with their start and end apart: 27 -> 27, of which waited for: 20 -> 19; matrix products, arithmetic and copies ran while one was open for 4% -> 4% of each run, Pallas kernels for 6% -> 6%
where the time goes in v3:
time: 202 us
  waiting for transfers between devices  87.1 us (43%)
  starting transfers between devices  68 us (34%)
  Pallas kernels  21.9 us (11%)
  local copies, waits for them, and re-layouts  16.4 us (8%)
  other arithmetic  4.79 us (2%)
  between operations  3.4 us (2%)
    ppermute x26, waiting for transfers between devices, permute(): lax.ppermute(value, axis, [(s, target(s)) for s in range(lax.axis_size(ax...  76.5 us
    ppermute x26, starting transfers between devices, permute(): lax.ppermute(value, axis, [(s, target(s)) for s in range(lax.axis_size(ax...  55.8 us
    pallas_call x3, Pallas kernels, product(): pl.pallas_call(functools.partial(product_kernel, jobs, len(left), len(rig...  18 us
    all_to_all x1, starting transfers between devices, body(): lax.all_to_all(swapped, ALL, split_axis=0, concat_axis=0, tiled=True)  12.2 us
    all_to_all x1, waiting for transfers between devices, body(): lax.all_to_all(swapped, ALL, split_axis=0, concat_axis=0, tiled=True)  10.6 us
    unnamed x29, local copies, waits for them, and re-layouts  5.75 us
  transfers between devices with their start and end apart: 27, of which 19 were waited for; matrix products, arithmetic and copies ran while one was open for 4% of the time, Pallas kernels for 6%

profile of v3, /device:TPU:1, one launch (start us, length us, event | category | flops | bytes accessed | tf_op | source)
XLA Modules:
  0.0 201.5 jit_solution(5624800660040369286)
XLA Ops:
  0.0 3.6 %collective-permute-start = (bf16[4,640,640]{2,1,0:T(8,128)(2,1)}, bf16[4,640,640]{2,1,0:T(8,128)(2,1)}, u32[]{:S(2)}, u32[]{:S(2)}) collective-permute-start(bf16[4,640,640]{2,1,0:T(8,128)(2,1)} %bitcast.206), channel_id=1, source_target_pairs={{0,3},{1,2},{2,1},{3,0},{4,7},{5,6},{6,5},{7,4},{8,11},{9,10},{10,... | collective-permute-start | bytes 9830408 | tf_op jit(solution)/shard_map/ppermute | solution.py:17
  4.6 1.9 copy-done.2
  6.5 2.2 %shard_map.64.refs_0_ = bf16[5,4,128,640]{3,2,1,0:T(8,128)(2,1)S(1)} custom-call(bf16[2,5,4,640]{3,2,1,0:T(4,128)(2,1)S(1)} %convert_element_type.34.mask_ref, bf16[2,2,8,5,4,4,640]{6,5,4,3,2,1,0:T(4,128)(2,1)S(1)} %bitcast.209), custom_call_target="tpu_custom_call" | custom-call | flops 1 | bytes 1 | tf_op jit(solution)/shard_map/pallas_call | solution.py:41
  10.8 4.0 %shard_map.65 = (f32[4,25,16,128]{3,2,1,0:T(8,128)S(1)}, f32[4,25,16,128]{3,2,1,0:T(8,128)}) custom-call(s32[1]{0:T(128)} %bitcast.6.core_ref, bf16[5,4,128,640]{3,2,1,0:T(8,128)(2,1)S(1)} %shard_map.64.refs_0_, bf16[4,640,640]{2,1,0:T(8,128)(2,1)S(1)} %bitcast.207), custom_call_target="tpu_custom_call" | custom-call | flops 1 | bytes 1 | tf_op jit(solution)/shard_map/pallas_call | solution.py:95
  23.3 2.5 %collective-permute-start.3 = (f32[25,16,128]{2,1,0:T(8,128)S(1)}, f32[25,16,128]{2,1,0:T(8,128)S(1)}, u32[]{:S(2)}, u32[]{:S(2)}) collective-permute-start(f32[25,16,128]{2,1,0:T(8,128)S(1)} %get-tuple-element.44), channel_id=1, source_target_pairs={{0,16},{8,24},{16,0},{24,8},{1,17},{9,25},{17,1},{25,9},{2,18},{10... | collective-permute-start | bytes 614408 | tf_op jit(solution)/shard_map/ppermute | solution.py:17
  26.9 3.2 %collective-permute-done.2 = f32[25,16,128]{2,1,0:T(8,128)S(1)} collective-permute-done((f32[25,16,128]{2,1,0:T(8,128)S(1)}, f32[25,16,128]{2,1,0:T(8,128)S(1)}, u32[]{:S(2)}, u32[]{:S(2)}) %collective-permute-start.2) | collective-permute-done | bytes 204832 | tf_op jit(solution)/shard_map/ppermute | solution.py:17
  30.1 5.3 %collective-permute-done.3 = f32[25,16,128]{2,1,0:T(8,128)S(1)} collective-permute-done((f32[25,16,128]{2,1,0:T(8,128)S(1)}, f32[25,16,128]{2,1,0:T(8,128)S(1)}, u32[]{:S(2)}, u32[]{:S(2)}) %collective-permute-start.3) | collective-permute-done | bytes 204832 | tf_op jit(solution)/shard_map/ppermute | solution.py:17
  38.3 2.7 %collective-permute-done.5 = f32[2,2,50,128]{3,2,1,0:T(8,128)S(1)} collective-permute-done((f32[2,2,50,128]{3,2,1,0:T(8,128)S(1)}, f32[2,2,50,128]{3,2,1,0:T(8,128)S(1)}, u32[]{:S(2)}, u32[]{:S(2)}) %collective-permute-start.5) | collective-permute-done | bytes 102432 | tf_op jit(solution)/shard_map/ppermute | solution.py:17
  41.0 3.1 %collective-permute-start.6 = (f32[2,50,128]{2,1,0:T(8,128)S(1)}, f32[2,50,128]{2,1,0:T(8,128)S(1)}, u32[]{:S(2)}, u32[]{:S(2)}) collective-permute-start(f32[2,50,128]{2,1,0:T(8,128)S(1)} %dynamic-slice_bitcast_fusion.4), channel_id=1, source_target_pairs={{0,64},{64,0},{1,65},{65,1},{2,66},{66,2},{3,67},{67,3},{4,68},{68... | collective-permute-start | bytes 153608 | tf_op jit(solution)/shard_map/ppermute | solution.py:17
  46.7 26.7 %collective-permute-done.refs_1_.refs_2_ = bf16[4,640,640]{2,1,0:T(8,128)(2,1)} collective-permute-done((bf16[4,640,640]{2,1,0:T(8,128)(2,1)}, bf16[4,640,640]{2,1,0:T(8,128)(2,1)}, u32[]{:S(2)}, u32[]{:S(2)}) %collective-permute-start) | collective-permute-done | bytes 3276832 | tf_op jit(solution)/shard_map/ppermute | solution.py:17
  73.5 5.1 %shard_map.66 = (f32[4,25,16,128]{3,2,1,0:T(8,128)S(1)}, f32[4,25,16,128]{3,2,1,0:T(8,128)S(1)}) custom-call(s32[1]{0:T(128)} %bitcast.6.core_ref, bf16[5,4,128,640]{3,2,1,0:T(8,128)(2,1)S(1)} %shard_map.64.refs_0_, bf16[4,640,640]{2,1,0:T(8,128)(2,1)} %collective-permute-done.refs_1_.refs_2_), custom_call_target="tpu_custom_call" | custom-call | flops 1 | bytes 1 | tf_op jit(solution)/shard_map/pallas_call | solution.py:95
  78.6 2.5 %collective-permute-start.8 = (f32[4,25,16,128]{3,2,1,0:T(8,128)S(1)}, f32[4,25,16,128]{3,2,1,0:T(8,128)S(1)}, u32[]{:S(2)}, u32[]{:S(2)}) collective-permute-start(f32[4,25,16,128]{3,2,1,0:T(8,128)S(1)} %get-tuple-element.22), channel_id=1, source_target_pairs={{0,4},{4,0},{1,5},{5,1},{2,6},{6,2},{3,7},{7,3},{8,12},{12,8},{9,1... | collective-permute-start | bytes 2457608 | tf_op jit(solution)/shard_map/ppermute | solution.py:17
  81.2 2.0 collective-permute-done.8
  83.1 8.9 %shard_map.67 = (f32[4,50,16,128]{3,2,1,0:T(8,128)S(1)}, f32[4,50,16,128]{3,2,1,0:T(8,128)S(1)}) custom-call(s32[1]{0:T(128)} %bitcast.6.core_ref, bf16[5,4,128,640]{3,2,1,0:T(8,128)(2,1)} %collective-permute-done.12.refs_0_, bf16[4,640,640]{2,1,0:T(8,128)(2,1)S(1)} %bitcast.208, bf16[4,640,640]{2,1,0:T(8,128)(2,1)} %collective-permute-done.refs_1_.refs_2_), custom_call_target="tpu_custom_call" | custom-call | flops 1 | bytes 1 | tf_op jit(solution)/shard_map/pallas_call | solution.py:95
  92.6 2.8 %collective-permute-start.10 = (f32[25,16,128]{2,1,0:T(8,128)S(1)}, f32[25,16,128]{2,1,0:T(8,128)S(1)}, u32[]{:S(2)}, u32[]{:S(2)}) collective-permute-start(f32[25,16,128]{2,1,0:T(8,128)S(1)} %get-tuple-element.41), channel_id=1, source_target_pairs={{0,16},{8,24},{16,0},{24,8},{1,17},{9,25},{17,1},{25,9},{2,18},{10... | collective-permute-start | bytes 614408 | tf_op jit(solution)/shard_map/ppermute | solution.py:17
  97.4 2.9 %collective-permute-start.15 = (f32[50,16,128]{2,1,0:T(8,128)S(1)}, f32[50,16,128]{2,1,0:T(8,128)S(1)}, u32[]{:S(2)}, u32[]{:S(2)}) collective-permute-start(f32[50,16,128]{2,1,0:T(8,128)S(1)} %get-tuple-element.38), channel_id=1, source_target_pairs={{0,16},{8,24},{16,0},{24,8},{1,17},{9,25},{17,1},{25,9},{2,18},{10... | collective-permute-start | bytes 1228808 | tf_op jit(solution)/shard_map/ppermute | solution.py:17
  100.7 2.5 %collective-permute-start.16 = (f32[50,16,128]{2,1,0:T(8,128)S(1)}, f32[50,16,128]{2,1,0:T(8,128)S(1)}, u32[]{:S(2)}, u32[]{:S(2)}) collective-permute-start(f32[50,16,128]{2,1,0:T(8,128)S(1)} %get-tuple-element.37), channel_id=1, source_target_pairs={{0,24},{8,0},{16,8},{24,16},{1,25},{9,1},{17,9},{25,17},{2,26},{10... | collective-permute-start | bytes 1228808 | tf_op jit(solution)/shard_map/ppermute | solution.py:17
  103.2 2.0 collective-permute-done.11
  105.4 8.9 %collective-permute-done.14 = f32[50,16,128]{2,1,0:T(8,128)S(1)} collective-permute-done((f32[50,16,128]{2,1,0:T(8,128)S(1)}, f32[50,16,128]{2,1,0:T(8,128)S(1)}, u32[]{:S(2)}, u32[]{:S(2)}) %collective-permute-start.14) | collective-permute-done | bytes 409632 | tf_op jit(solution)/shard_map/ppermute | solution.py:17
  114.3 8.3 %collective-permute-done.15 = f32[50,16,128]{2,1,0:T(8,128)S(1)} collective-permute-done((f32[50,16,128]{2,1,0:T(8,128)S(1)}, f32[50,16,128]{2,1,0:T(8,128)S(1)}, u32[]{:S(2)}, u32[]{:S(2)}) %collective-permute-start.15) | collective-permute-done | bytes 409632 | tf_op jit(solution)/shard_map/ppermute | solution.py:17
  125.0 6.6 %collective-permute-done.17 = f32[2,2,150,128]{3,2,1,0:T(8,128)S(1)} collective-permute-done((f32[2,2,150,128]{3,2,1,0:T(8,128)S(1)}, f32[2,2,150,128]{3,2,1,0:T(8,128)S(1)}, u32[]{:S(2)}, u32[]{:S(2)}) %collective-permute-start.17) | collective-permute-done | bytes 307232 | tf_op jit(solution)/shard_map/ppermute | solution.py:17
  131.7 3.1 %collective-permute-start.18 = (f32[2,150,128]{2,1,0:T(8,128)S(1)}, f32[2,150,128]{2,1,0:T(8,128)S(1)}, u32[]{:S(2)}, u32[]{:S(2)}) collective-permute-start(f32[2,150,128]{2,1,0:T(8,128)S(1)} %dynamic-slice_bitcast_fusion), channel_id=1, source_target_pairs={{0,64},{64,0},{1,65},{65,1},{2,66},{66,2},{3,67},{67,3},{4,68},{68... | collective-permute-start | bytes 460808 | tf_op jit(solution)/shard_map/ppermute | solution.py:17
  134.8 4.7 %collective-permute-start.7 = (f32[50,128]{1,0:T(8,128)S(1)}, f32[50,128]{1,0:T(8,128)S(1)}, u32[]{:S(2)}, u32[]{:S(2)}) collective-permute-start(f32[50,128]{1,0:T(8,128)S(1)} %get-tuple-element.74), channel_id=1, source_target_pairs={{0,128},{128,0},{1,129},{129,1},{2,130},{130,2},{3,131},{131,3},{4... | collective-permute-start | bytes 76808 | tf_op jit(solution)/shard_map/ppermute | solution.py:17
  139.5 2.1 %collective-permute-done.18 = f32[2,150,128]{2,1,0:T(8,128)S(1)} collective-permute-done((f32[2,150,128]{2,1,0:T(8,128)S(1)}, f32[2,150,128]{2,1,0:T(8,128)S(1)}, u32[]{:S(2)}, u32[]{:S(2)}) %collective-permute-start.18) | collective-permute-done | bytes 153632 | tf_op jit(solution)/shard_map/ppermute | solution.py:17
  142.3 7.3 %collective-permute-start.19 = (f32[150,128]{1,0:T(8,128)S(1)}, f32[150,128]{1,0:T(8,128)S(1)}, u32[]{:S(2)}, u32[]{:S(2)}) collective-permute-start(f32[150,128]{1,0:T(8,128)S(1)} %get-tuple-element.68), channel_id=1, source_target_pairs={{0,128},{128,0},{1,129},{129,1},{2,130},{130,2},{3,131},{131,3},{4... | collective-permute-start | bytes 230408 | tf_op jit(solution)/shard_map/ppermute | solution.py:17
  156.1 2.8 %collective-permute-start.20 = (f32[20,640]{1,0:T(8,128)S(1)}, f32[20,640]{1,0:T(8,128)S(1)}, u32[]{:S(2)}, u32[]{:S(2)}) collective-permute-start(f32[20,640]{1,0:T(8,128)S(1)} %squeeze.151), channel_id=1, source_target_pairs={{0,3},{1,0},{2,1},{3,2},{4,7},{5,4},{6,5},{7,6},{8,11},{9,8},{10,9... | collective-permute-start | bytes 153608 | tf_op jit(solution)/shard_map/ppermute | solution.py:17
  160.2 3.5 %collective-permute-done.21 = f32[20,640]{1,0:T(8,128)S(1)} collective-permute-done((f32[20,640]{1,0:T(8,128)S(1)}, f32[20,640]{1,0:T(8,128)S(1)}, u32[]{:S(2)}, u32[]{:S(2)}) %collective-permute-start.21) | collective-permute-done | bytes 51232 | tf_op jit(solution)/shard_map/ppermute | solution.py:17
  167.0 2.7 %collective-permute-start.23 = (f32[5,1280]{1,0:T(8,128)S(1)}, f32[5,1280]{1,0:T(8,128)S(1)}, u32[]{:S(2)}, u32[]{:S(2)}) collective-permute-start(f32[5,1280]{1,0:T(8,128)S(1)} %bitcast.225), channel_id=1, source_target_pairs={{0,192},{64,0},{128,64},{192,128},{1,193},{65,1},{129,65},{193,129... | collective-permute-start | bytes 76808 | tf_op jit(solution)/shard_map/ppermute | solution.py:17
  169.7 2.9 %collective-permute-start.24 = (f32[5,1280]{1,0:T(8,128)S(1)}, f32[5,1280]{1,0:T(8,128)S(1)}, u32[]{:S(2)}, u32[]{:S(2)}) collective-permute-start(f32[5,1280]{1,0:T(8,128)S(1)} %bitcast.226), channel_id=1, source_target_pairs={{0,128},{64,192},{128,0},{192,64},{1,129},{65,193},{129,1},{193,65... | collective-permute-start | bytes 76808 | tf_op jit(solution)/shard_map/ppermute | solution.py:17
  172.6 2.3 %collective-permute-start.25 = (f32[5,1280]{1,0:T(8,128)S(1)}, f32[5,1280]{1,0:T(8,128)S(1)}, u32[]{:S(2)}, u32[]{:S(2)}) collective-permute-start(f32[5,1280]{1,0:T(8,128)S(1)} %bitcast.227), channel_id=1, source_target_pairs={{0,64},{64,128},{128,192},{192,0},{1,65},{65,129},{129,193},{193,1... | collective-permute-start | bytes 76808 | tf_op jit(solution)/shard_map/ppermute | solution.py:17
  175.6 12.2 %all-to-all-start = ((f32[64,1,400]{2,1,0:T(1,128)}), f32[64,1,400]{2,1,0:T(1,128)S(1)}, u32[]{:S(2)}, u32[]{:S(2)}) async-start(f32[64,1,400]{2,1,0:T(1,128)} %copy.659), calls=%async_computation | async-start | bytes 262144 | tf_op jit(solution)/shard_map/all_to_all | solution.py:229
  188.3 10.6 %all-to-all-done = f32[64,1,400]{2,1,0:T(1,128)S(1)} async-done(((f32[64,1,400]{2,1,0:T(1,128)}), f32[64,1,400]{2,1,0:T(1,128)S(1)}, u32[]{:S(2)}, u32[]{:S(2)}) %all-to-all-start) | async-done | bytes 102432 | tf_op jit(solution)/shard_map/all_to_all | solution.py:229
  (131 shorter events, 36.2 us)
Async XLA Ops:
  0.0 73.5 %collective-permute-start = (bf16[4,640,640]{2,1,0:T(8,128)(2,1)}, bf16[4,640,640]{2,1,0:T(8,128)(2,1)}, u32[]{:S(2)}, u32[]{:S(2)}) collective-permute-start(bf16[4,640,640]{2,1,0:T(8,128)(2,1)} %bitcast.206), channel_id=1, source_target_pairs={{0,3},{1,2},{2,1},{3,0},{4,7},{5,6},{6,5},{7,4},{8,11},{9,10},{10,... | collective-permute-start | bytes 9830408 | tf_op jit(solution)/shard_map/ppermute | solution.py:17
  4.6 1.9 copy-start.2
  8.8 72.4 %collective-permute-start.12 = (bf16[5,4,128,640]{3,2,1,0:T(8,128)(2,1)S(1)}, bf16[5,4,128,640]{3,2,1,0:T(8,128)(2,1)}, u32[]{:S(2)}, u32[]{:S(2)}) collective-permute-start(bf16[5,4,128,640]{3,2,1,0:T(8,128)(2,1)S(1)} %shard_map.64.refs_0_), channel_id=1, source_target_pairs={{0,1},{1,0},{2,3},{3,2},{4,5},{5,4},{6,7},{7,6},{8,9},{9,8},{10,11... | collective-permute-start | bytes 9830408 | tf_op jit(solution)/shard_map/ppermute | solution.py:17
  10.8 6.0 %copy-start.8 = (s32[4]{0:T(128)S(1)}, s32[4]{0:T(128)}, u32[]{:S(2)}) copy-start(s32[4]{0:T(128)} %param.11) | copy-start | bytes 52
  10.8 6.3 %copy-start.7 = (f32[2]{0:T(128)S(1)}, f32[2]{0:T(128)}, u32[]{:S(2)}) copy-start(f32[2]{0:T(128)} %param.9) | copy-start | bytes 28
  15.7 4.8 %collective-permute-start.1 = (f32[4,25,16,128]{3,2,1,0:T(8,128)}, f32[4,25,16,128]{3,2,1,0:T(8,128)}, u32[]{:S(2)}, u32[]{:S(2)}) collective-permute-start(f32[4,25,16,128]{3,2,1,0:T(8,128)} %get-tuple-element.18), channel_id=1, source_target_pairs={{0,4},{4,0},{1,5},{5,1},{2,6},{6,2},{3,7},{7,3},{8,12},{12,8},{9,1... | collective-permute-start | bytes 2457608 | tf_op jit(solution)/shard_map/ppermute | solution.py:17
  20.5 23.6 %copy-start.6 = (f32[1280]{0:T(1024)S(1)}, f32[1280]{0:T(1024)}, u32[]{:S(2)}) copy-start(f32[1280]{0:T(1024)} %param.10) | copy-start | bytes 15364
  22.0 8.1 %collective-permute-start.2 = (f32[25,16,128]{2,1,0:T(8,128)S(1)}, f32[25,16,128]{2,1,0:T(8,128)S(1)}, u32[]{:S(2)}, u32[]{:S(2)}) collective-permute-start(f32[25,16,128]{2,1,0:T(8,128)S(1)} %get-tuple-element.42), channel_id=1, source_target_pairs={{0,8},{8,16},{16,24},{24,0},{1,9},{9,17},{17,25},{25,1},{2,10},{10... | collective-permute-start | bytes 614408 | tf_op jit(solution)/shard_map/ppermute | solution.py:17
  23.3 12.1 %collective-permute-start.3 = (f32[25,16,128]{2,1,0:T(8,128)S(1)}, f32[25,16,128]{2,1,0:T(8,128)S(1)}, u32[]{:S(2)}, u32[]{:S(2)}) collective-permute-start(f32[25,16,128]{2,1,0:T(8,128)S(1)} %get-tuple-element.44), channel_id=1, source_target_pairs={{0,16},{8,24},{16,0},{24,8},{1,17},{9,25},{17,1},{25,9},{2,18},{10... | collective-permute-start | bytes 614408 | tf_op jit(solution)/shard_map/ppermute | solution.py:17
  25.7 9.6 %collective-permute-start.4 = (f32[25,16,128]{2,1,0:T(8,128)S(1)}, f32[25,16,128]{2,1,0:T(8,128)S(1)}, u32[]{:S(2)}, u32[]{:S(2)}) collective-permute-start(f32[25,16,128]{2,1,0:T(8,128)S(1)} %get-tuple-element.43), channel_id=1, source_target_pairs={{0,24},{8,0},{16,8},{24,16},{1,25},{9,1},{17,9},{25,17},{2,26},{10... | collective-permute-start | bytes 614408 | tf_op jit(solution)/shard_map/ppermute | solution.py:17
  36.5 4.5 %collective-permute-start.5 = (f32[2,2,50,128]{3,2,1,0:T(8,128)S(1)}, f32[2,2,50,128]{3,2,1,0:T(8,128)S(1)}, u32[]{:S(2)}, u32[]{:S(2)}) collective-permute-start(f32[2,2,50,128]{3,2,1,0:T(8,128)S(1)} %bitcast.224), channel_id=1, source_target_pairs={{0,32},{32,0},{1,33},{33,1},{2,34},{34,2},{3,35},{35,3},{4,36},{36... | collective-permute-start | bytes 307208 | tf_op jit(solution)/shard_map/ppermute | solution.py:17
  41.0 5.1 %collective-permute-start.6 = (f32[2,50,128]{2,1,0:T(8,128)S(1)}, f32[2,50,128]{2,1,0:T(8,128)S(1)}, u32[]{:S(2)}, u32[]{:S(2)}) collective-permute-start(f32[2,50,128]{2,1,0:T(8,128)S(1)} %dynamic-slice_bitcast_fusion.4), channel_id=1, source_target_pairs={{0,64},{64,0},{1,65},{65,1},{2,66},{66,2},{3,67},{67,3},{4,68},{68... | collective-permute-start | bytes 153608 | tf_op jit(solution)/shard_map/ppermute | solution.py:17
  73.5 9.7 %copy-start.1 = (bf16[4,640,2,320]{1,3,2,0:T(8,128)(2,1)S(1)}, bf16[4,640,2,320]{1,3,2,0:T(8,128)(2,1)}, u32[]{:S(2)}) copy-start(bf16[4,640,2,320]{1,3,2,0:T(8,128)(2,1)} %param.7) | copy-start | bytes 9830404
  78.6 4.5 %collective-permute-start.8 = (f32[4,25,16,128]{3,2,1,0:T(8,128)S(1)}, f32[4,25,16,128]{3,2,1,0:T(8,128)S(1)}, u32[]{:S(2)}, u32[]{:S(2)}) collective-permute-start(f32[4,25,16,128]{3,2,1,0:T(8,128)S(1)} %get-tuple-element.22), channel_id=1, source_target_pairs={{0,4},{4,0},{1,5},{5,1},{2,6},{6,2},{3,7},{7,3},{8,12},{12,8},{9,1... | collective-permute-start | bytes 2457608 | tf_op jit(solution)/shard_map/ppermute | solution.py:17
  92.0 4.9 %collective-permute-start.13 = (f32[4,50,16,128]{3,2,1,0:T(8,128)S(1)}, f32[4,50,16,128]{3,2,1,0:T(8,128)S(1)}, u32[]{:S(2)}, u32[]{:S(2)}) collective-permute-start(f32[4,50,16,128]{3,2,1,0:T(8,128)S(1)} %get-tuple-element.25), channel_id=1, source_target_pairs={{0,4},{4,0},{1,5},{5,1},{2,6},{6,2},{3,7},{7,3},{8,12},{12,8},{9,1... | collective-permute-start | bytes 4915208 | tf_op jit(solution)/shard_map/ppermute | solution.py:17
  92.6 8.1 %collective-permute-start.10 = (f32[25,16,128]{2,1,0:T(8,128)S(1)}, f32[25,16,128]{2,1,0:T(8,128)S(1)}, u32[]{:S(2)}, u32[]{:S(2)}) collective-permute-start(f32[25,16,128]{2,1,0:T(8,128)S(1)} %get-tuple-element.41), channel_id=1, source_target_pairs={{0,16},{8,24},{16,0},{24,8},{1,17},{9,25},{17,1},{25,9},{2,18},{10... | collective-permute-start | bytes 614408 | tf_op jit(solution)/shard_map/ppermute | solution.py:17
  95.4 9.8 %collective-permute-start.11 = (f32[25,16,128]{2,1,0:T(8,128)S(1)}, f32[25,16,128]{2,1,0:T(8,128)S(1)}, u32[]{:S(2)}, u32[]{:S(2)}) collective-permute-start(f32[25,16,128]{2,1,0:T(8,128)S(1)} %get-tuple-element.40), channel_id=1, source_target_pairs={{0,24},{8,0},{16,8},{24,16},{1,25},{9,1},{17,9},{25,17},{2,26},{10... | collective-permute-start | bytes 614408 | tf_op jit(solution)/shard_map/ppermute | solution.py:17
  96.3 9.1 %collective-permute-start.9 = (f32[25,16,128]{2,1,0:T(8,128)S(1)}, f32[25,16,128]{2,1,0:T(8,128)S(1)}, u32[]{:S(2)}, u32[]{:S(2)}) collective-permute-start(f32[25,16,128]{2,1,0:T(8,128)S(1)} %get-tuple-element.39), channel_id=1, source_target_pairs={{0,8},{8,16},{16,24},{24,0},{1,9},{9,17},{17,25},{25,1},{2,10},{10... | collective-permute-start | bytes 614408 | tf_op jit(solution)/shard_map/ppermute | solution.py:17
  97.0 17.3 %collective-permute-start.14 = (f32[50,16,128]{2,1,0:T(8,128)S(1)}, f32[50,16,128]{2,1,0:T(8,128)S(1)}, u32[]{:S(2)}, u32[]{:S(2)}) collective-permute-start(f32[50,16,128]{2,1,0:T(8,128)S(1)} %get-tuple-element.36), channel_id=1, source_target_pairs={{0,8},{8,16},{16,24},{24,0},{1,9},{9,17},{17,25},{25,1},{2,10},{10... | collective-permute-start | bytes 1228808 | tf_op jit(solution)/shard_map/ppermute | solution.py:17
  97.4 25.2 %collective-permute-start.15 = (f32[50,16,128]{2,1,0:T(8,128)S(1)}, f32[50,16,128]{2,1,0:T(8,128)S(1)}, u32[]{:S(2)}, u32[]{:S(2)}) collective-permute-start(f32[50,16,128]{2,1,0:T(8,128)S(1)} %get-tuple-element.38), channel_id=1, source_target_pairs={{0,16},{8,24},{16,0},{24,8},{1,17},{9,25},{17,1},{25,9},{2,18},{10... | collective-permute-start | bytes 1228808 | tf_op jit(solution)/shard_map/ppermute | solution.py:17
  100.7 22.1 %collective-permute-start.16 = (f32[50,16,128]{2,1,0:T(8,128)S(1)}, f32[50,16,128]{2,1,0:T(8,128)S(1)}, u32[]{:S(2)}, u32[]{:S(2)}) collective-permute-start(f32[50,16,128]{2,1,0:T(8,128)S(1)} %get-tuple-element.37), channel_id=1, source_target_pairs={{0,24},{8,0},{16,8},{24,16},{1,25},{9,1},{17,9},{25,17},{2,26},{10... | collective-permute-start | bytes 1228808 | tf_op jit(solution)/shard_map/ppermute | solution.py:17
  123.3 8.4 %collective-permute-start.17 = (f32[2,2,150,128]{3,2,1,0:T(8,128)S(1)}, f32[2,2,150,128]{3,2,1,0:T(8,128)S(1)}, u32[]{:S(2)}, u32[]{:S(2)}) collective-permute-start(f32[2,2,150,128]{3,2,1,0:T(8,128)S(1)} %bitcast.219), channel_id=1, source_target_pairs={{0,32},{32,0},{1,33},{33,1},{2,34},{34,2},{3,35},{35,3},{4,36},{36... | collective-permute-start | bytes 921608 | tf_op jit(solution)/shard_map/ppermute | solution.py:17
  131.7 9.9 %collective-permute-start.18 = (f32[2,150,128]{2,1,0:T(8,128)S(1)}, f32[2,150,128]{2,1,0:T(8,128)S(1)}, u32[]{:S(2)}, u32[]{:S(2)}) collective-permute-start(f32[2,150,128]{2,1,0:T(8,128)S(1)} %dynamic-slice_bitcast_fusion), channel_id=1, source_target_pairs={{0,64},{64,0},{1,65},{65,1},{2,66},{66,2},{3,67},{67,3},{4,68},{68... | collective-permute-start | bytes 460808 | tf_op jit(solution)/shard_map/ppermute | solution.py:17
  134.8 14.8 %collective-permute-start.7 = (f32[50,128]{1,0:T(8,128)S(1)}, f32[50,128]{1,0:T(8,128)S(1)}, u32[]{:S(2)}, u32[]{:S(2)}) collective-permute-start(f32[50,128]{1,0:T(8,128)S(1)} %get-tuple-element.74), channel_id=1, source_target_pairs={{0,128},{128,0},{1,129},{129,1},{2,130},{130,2},{3,131},{131,3},{4... | collective-permute-start | bytes 76808 | tf_op jit(solution)/shard_map/ppermute | solution.py:17
  142.3 9.1 %collective-permute-start.19 = (f32[150,128]{1,0:T(8,128)S(1)}, f32[150,128]{1,0:T(8,128)S(1)}, u32[]{:S(2)}, u32[]{:S(2)}) collective-permute-start(f32[150,128]{1,0:T(8,128)S(1)} %get-tuple-element.68), channel_id=1, source_target_pairs={{0,128},{128,0},{1,129},{129,1},{2,130},{130,2},{3,131},{131,3},{4... | collective-permute-start | bytes 230408 | tf_op jit(solution)/shard_map/ppermute | solution.py:17
  156.1 4.1 %collective-permute-start.20 = (f32[20,640]{1,0:T(8,128)S(1)}, f32[20,640]{1,0:T(8,128)S(1)}, u32[]{:S(2)}, u32[]{:S(2)}) collective-permute-start(f32[20,640]{1,0:T(8,128)S(1)} %squeeze.151), channel_id=1, source_target_pairs={{0,3},{1,0},{2,1},{3,2},{4,7},{5,4},{6,5},{7,6},{8,11},{9,8},{10,9... | collective-permute-start | bytes 153608 | tf_op jit(solution)/shard_map/ppermute | solution.py:17
  158.9 4.8 %collective-permute-start.21 = (f32[20,640]{1,0:T(8,128)S(1)}, f32[20,640]{1,0:T(8,128)S(1)}, u32[]{:S(2)}, u32[]{:S(2)}) collective-permute-start(f32[20,640]{1,0:T(8,128)S(1)} %squeeze.152), channel_id=1, source_target_pairs={{0,2},{1,3},{2,0},{3,1},{4,6},{5,7},{6,4},{7,5},{8,10},{9,11},{10,... | collective-permute-start | bytes 153608 | tf_op jit(solution)/shard_map/ppermute | solution.py:17
  159.0 5.0 %collective-permute-start.22 = (f32[20,640]{1,0:T(8,128)S(1)}, f32[20,640]{1,0:T(8,128)S(1)}, u32[]{:S(2)}, u32[]{:S(2)}) collective-permute-start(f32[20,640]{1,0:T(8,128)S(1)} %squeeze.153), channel_id=1, source_target_pairs={{0,1},{1,2},{2,3},{3,0},{4,5},{5,6},{6,7},{7,4},{8,9},{9,10},{10,1... | collective-permute-start | bytes 153608 | tf_op jit(solution)/shard_map/ppermute | solution.py:17
  167.0 20.8 %collective-permute-start.23 = (f32[5,1280]{1,0:T(8,128)S(1)}, f32[5,1280]{1,0:T(8,128)S(1)}, u32[]{:S(2)}, u32[]{:S(2)}) collective-permute-start(f32[5,1280]{1,0:T(8,128)S(1)} %bitcast.225), channel_id=1, source_target_pairs={{0,192},{64,0},{128,64},{192,128},{1,193},{65,1},{129,65},{193,129... | collective-permute-start | bytes 76808 | tf_op jit(solution)/shard_map/ppermute | solution.py:17
  169.7 18.1 %collective-permute-start.24 = (f32[5,1280]{1,0:T(8,128)S(1)}, f32[5,1280]{1,0:T(8,128)S(1)}, u32[]{:S(2)}, u32[]{:S(2)}) collective-permute-start(f32[5,1280]{1,0:T(8,128)S(1)} %bitcast.226), channel_id=1, source_target_pairs={{0,128},{64,192},{128,0},{192,64},{1,129},{65,193},{129,1},{193,65... | collective-permute-start | bytes 76808 | tf_op jit(solution)/shard_map/ppermute | solution.py:17
  172.6 15.3 %collective-permute-start.25 = (f32[5,1280]{1,0:T(8,128)S(1)}, f32[5,1280]{1,0:T(8,128)S(1)}, u32[]{:S(2)}, u32[]{:S(2)}) collective-permute-start(f32[5,1280]{1,0:T(8,128)S(1)} %bitcast.227), channel_id=1, source_target_pairs={{0,64},{64,128},{128,192},{192,0},{1,65},{65,129},{129,193},{193,1... | collective-permute-start | bytes 76808 | tf_op jit(solution)/shard_map/ppermute | solution.py:17
  175.6 23.3 %all-to-all-start = ((f32[64,1,400]{2,1,0:T(1,128)}), f32[64,1,400]{2,1,0:T(1,128)S(1)}, u32[]{:S(2)}, u32[]{:S(2)}) async-start(f32[64,1,400]{2,1,0:T(1,128)} %copy.659), calls=%async_computation | async-start | bytes 262144 | tf_op jit(solution)/shard_map/all_to_all | solution.py:229
  (4 other events, 5.3 us)
